TPU v7x, 256 devices: a whole 4x4x8 slice. The times are simulated.
256 devices in a mesh: dp: 4 (over y), expert: 64 (over x, z, core).
Axes of the slice: x: 4, y: 4, z: 8, core: 2. Of those that a mesh axis runs over, the one named last changes fastest.
Arguments:
- tokens: bfloat16 [8192, 2048], P(('dp', 'expert')), may hold values from -6 to 6
- expert_ids: int32 [8192, 8], P(('dp', 'expert')), may hold values from 0 to 63, all different within a row; in each aligned block of 32 rows (0 to 31, 32 to 63, ...) at most 8 rows name the same one
- gate_probs: float32 [8192, 8], P(('dp', 'expert')), may hold values from 0.1 to 1
- grad_out: bfloat16 [8192, 2048], P(('dp', 'expert')), may hold values from -1.1953125 to 1.1953125
- w_gate: bfloat16 [64, 2048, 768], P('expert', 'dp'), may hold values from -0.125 to 0.125
- w_up: bfloat16 [64, 2048, 768], P('expert', 'dp'), may hold values from -0.125 to 0.125
- w_down: bfloat16 [64, 768, 2048], P('expert', None, 'dp'), may hold values from -0.21875 to 0.21875
Outputs:
- layer_out: bfloat16 [8192, 2048], P(('dp', 'expert'))
- grad_tokens: bfloat16 [8192, 2048], P(('dp', 'expert'))
- grad_probs: float32 [8192, 8], P(('dp', 'expert'))
- grad_gate: bfloat16 [64, 2048, 768], P('expert', 'dp')
- grad_up: bfloat16 [64, 2048, 768], P('expert', 'dp')
- grad_down: bfloat16 [64, 768, 2048], P('expert', None, 'dp')
Inputs may be any that keep to these rules, and one draw needn't show every extreme that they name: `expert_ids`: each row names 8 different experts. Within the 32 rows of one device no expert is named by more than 8 rows, a bound that some of them reach.
All inputs are finite; a program needn't handle non-finite values.
Results may differ from a plain program's by a relative error of at most 0.0064.
Values may be sent and summed in bfloat16 or wider, within the bound.
No kernel may reach another device: no remote copies, remote signals or barrier semaphores. Data moves between devices by JAX's collectives and lax.ppermute only.
A program may use at most 128 MiB of HBM per device.

v0:
```python
import jax
import jax.numpy as jnp
from jax import lax
from jax.sharding import PartitionSpec as P


def silu_parts(gate_vals):
    sig_vals = jax.nn.sigmoid(gate_vals)
    return (gate_vals * sig_vals, sig_vals * (1.0 + gate_vals * (1.0 - sig_vals)))


def contract(left_side, right_side, left_dim, right_dim):
    return lax.dot_general(
        left_side,
        right_side,
        (((left_dim,), (right_dim,)), ((), ())),
        preferred_element_type=jnp.float32,
    )


def activate(gate_vals, up_vals):
    act_vals, slope_vals = silu_parts(gate_vals)
    return ((act_vals * up_vals).astype(jnp.bfloat16), act_vals, slope_vals)


def pre_grads(grad_hidden, up_vals, act_vals, slope_vals):
    grad_gate_pre = (grad_hidden * up_vals * slope_vals).astype(jnp.bfloat16)
    grad_up_pre = (grad_hidden * act_vals).astype(jnp.bfloat16)
    return (grad_gate_pre, grad_up_pre)


def body(tokens, expert_ids, gate_probs, grad_out, w_gate, w_up, w_down):
    owners = lax.axis_size("expert")
    tok_count, top_count = expert_ids.shape
    model_width = tokens.shape[1]
    per_owner = min(tok_count, 2 * tok_count * top_count // owners)
    slot_count = owners * per_owner
    pair_count = tok_count * top_count
    flat_ids = expert_ids.reshape(-1)
    onehot = (flat_ids[:, None] == jnp.arange(owners, dtype=jnp.int32)[None, :]).astype(jnp.int32)
    before = jnp.cumsum(onehot, axis=0) - onehot
    rank_in = jnp.sum(before * onehot, axis=1)
    placed = flat_ids * per_owner + rank_in
    slot_table = placed[None, :] == jnp.arange(slot_count, dtype=jnp.int32)[:, None]
    filled = jnp.any(slot_table, axis=1)
    source_token = jnp.sum(
        jnp.where(slot_table, jnp.arange(pair_count, dtype=jnp.int32)[None, :] // top_count, 0),
        axis=1,
    )
    source_weight = jnp.sum(jnp.where(slot_table, gate_probs.reshape(-1)[None, :], 0.0), axis=1)
    token_slots = jnp.where(filled[:, None], tokens[source_token], jnp.zeros((), tokens.dtype))
    cotangent_slots = (source_weight[:, None] * grad_out[source_token].astype(jnp.float32)).astype(
        jnp.bfloat16
    )
    gate_part = w_gate[0]
    up_part = w_up[0]
    down_part = w_down[0]
    gate_full, up_full, down_full = (
        lax.all_gather(gate_part, "dp", axis=0, tiled=True),
        lax.all_gather(up_part, "dp", axis=0, tiled=True),
        lax.all_gather(down_part, "dp", axis=1, tiled=True),
    )
    arrived = lax.all_to_all(token_slots, "expert", split_axis=0, concat_axis=0, tiled=True)
    gate_vals = contract(arrived, gate_full, 1, 0)
    up_vals = contract(arrived, up_full, 1, 0)
    hidden, act_vals, slope_vals = activate(gate_vals, up_vals)
    expert_out = contract(hidden, down_full, 1, 0).astype(jnp.bfloat16)
    expert_out, kept_state = (expert_out, (arrived, hidden, up_vals, act_vals, slope_vals))
    back_out = lax.all_to_all(expert_out, "expert", split_axis=0, concat_axis=0, tiled=True)
    arrived_grads = lax.all_to_all(
        cotangent_slots, "expert", split_axis=0, concat_axis=0, tiled=True
    )
    rows_in, hidden, up_vals, act_vals, slope_vals = kept_state
    grad_hidden = contract(arrived_grads, down_full, 1, 1)
    grad_gate_pre, grad_up_pre = pre_grads(grad_hidden, up_vals, act_vals, slope_vals)
    grad_pair = (
        contract(grad_gate_pre, gate_full, 1, 1) + contract(grad_up_pre, up_full, 1, 1)
    ).astype(jnp.bfloat16)
    weight_sums = (
        lax.psum_scatter(
            contract(rows_in, grad_gate_pre, 0, 0), "dp", scatter_dimension=0, tiled=True
        ),
        lax.psum_scatter(
            contract(rows_in, grad_up_pre, 0, 0), "dp", scatter_dimension=0, tiled=True
        ),
        lax.psum_scatter(
            contract(hidden, arrived_grads, 0, 0), "dp", scatter_dimension=1, tiled=True
        ),
    )
    grad_pair, weight_sums = (grad_pair, weight_sums)
    back_grads = lax.all_to_all(grad_pair, "expert", split_axis=0, concat_axis=0, tiled=True)
    out_pairs = back_out[placed].reshape(tok_count, top_count, model_width).astype(jnp.float32)
    layer_out = jnp.sum(out_pairs * gate_probs[:, :, None], axis=1).astype(jnp.bfloat16)
    grad_probs = jnp.sum(out_pairs * grad_out[:, None, :].astype(jnp.float32), axis=2)
    grad_tokens = jnp.sum(
        back_grads[placed].reshape(tok_count, top_count, model_width).astype(jnp.float32), axis=1
    ).astype(jnp.bfloat16)
    grad_gate = weight_sums[0].astype(jnp.bfloat16)[None]
    grad_up = weight_sums[1].astype(jnp.bfloat16)[None]
    grad_down = weight_sums[2].astype(jnp.bfloat16)[None]
    return (layer_out, grad_tokens, grad_probs, grad_gate, grad_up, grad_down)


def solution(mesh):
    return jax.shard_map(
        body,
        mesh=mesh,
        in_specs=(
            P(("dp", "expert"), None),
            P(("dp", "expert"), None),
            P(("dp", "expert"), None),
            P(("dp", "expert"), None),
            P("expert", "dp", None),
            P("expert", "dp", None),
            P("expert", None, "dp"),
        ),
        out_specs=(
            P(("dp", "expert"), None),
            P(("dp", "expert"), None),
            P(("dp", "expert"), None),
            P("expert", "dp", None),
            P("expert", "dp", None),
            P("expert", None, "dp"),
        ),
        check_vma=False,
    )
```

profile of v0, /device:TPU:1, one launch (start us, length us, event | category | flops | bytes accessed | tf_op | source)
XLA Modules:
  0.0 368.5 jit_solution(2942007896031787855)
XLA Ops:
  10.5 0.8 copy.31
  11.9 2.5 gather_fusion.2
  14.4 1.8 fusion
  16.1 13.2 %all-to-all-start.2 = ((bf16[64,8,2048]{2,1,0:T(8,128)(2,1)}), bf16[64,8,2048]{2,1,0:T(8,128)(2,1)}, u32[]{:S(2)}, u32[]{:S(2)}) async-start(bf16[64,8,2048]{2,1,0:T(8,128)(2,1)} %fusion), calls=%async_computation.2 | async-start | bytes 4194304 | tf_op jit(solution)/shard_map/all_to_all | solution.py:70
  30.1 2.5 gather_fusion
  32.8 1.5 bitcast_select_fusion
  34.3 46.2 %all-to-all-done.2 = bf16[64,8,2048]{2,1,0:T(8,128)(2,1)} async-done(((bf16[64,8,2048]{2,1,0:T(8,128)(2,1)}), bf16[64,8,2048]{2,1,0:T(8,128)(2,1)}, u32[]{:S(2)}, u32[]{:S(2)}) %all-to-all-start.2) | async-done | bytes 2097184 | tf_op jit(solution)/shard_map/all_to_all | solution.py:70
  80.5 5.8 %all-to-all-start = ((bf16[64,8,2048]{2,1,0:T(8,128)(2,1)}), bf16[64,8,2048]{2,1,0:T(8,128)(2,1)S(1)}, u32[]{:S(2)}, u32[]{:S(2)}) async-start(bf16[64,8,2048]{2,1,0:T(8,128)(2,1)} %bitcast_select_fusion), calls=%async_computation | async-start | bytes 4194304 | tf_op jit(solution)/shard_map/all_to_all | solution.py:63
  86.5 5.6 %fusion.1 = f32[512,768]{1,0:T(8,128)} fusion(bf16[1,768,2048]{2,1,0:T(8,128)(2,1)} %all-gather.11.cloned.1.call-done, bf16[64,8,2048]{2,1,0:T(8,128)(2,1)} %all-to-all-done.2), kind=kOutput, calls=%fused_computation.7 | convolution fusion | flops 1610612736 | bytes 6815744 | tf_op jit(solution)/shard_map/dot_general | solution.py:13
  92.1 45.4 %all-to-all-done = bf16[64,8,2048]{2,1,0:T(8,128)(2,1)S(1)} async-done(((bf16[64,8,2048]{2,1,0:T(8,128)(2,1)}), bf16[64,8,2048]{2,1,0:T(8,128)(2,1)S(1)}, u32[]{:S(2)}, u32[]{:S(2)}) %all-to-all-start) | async-done | bytes 2097184 | tf_op jit(solution)/shard_map/all_to_all | solution.py:63
  137.5 4.8 %fusion.7 = f32[512,768]{1,0:T(8,128)} fusion(bf16[1,2048,768]{2,1,0:T(8,128)(2,1)} %all-gather.9.cloned.1.call-done, bf16[64,8,2048]{2,1,0:T(8,128)(2,1)S(1)} %all-to-all-done), kind=kOutput, calls=%fused_computation.13 | convolution fusion | flops 1610612736 | bytes 6815744 | tf_op jit(solution)/shard_map/dot_general | solution.py:13
  142.4 1.8 all-gather.7.cloned.1.call-done
  144.1 6.3 %multiply_convert_fusion.1 = (bf16[512,768]{1,0:T(8,128)(2,1)S(1)}, bf16[512,768]{1,0:T(8,128)(2,1)}, bf16[512,768]{1,0:T(8,128)(2,1)}) fusion(f32[512,768]{1,0:T(8,128)} %fusion.1, f32[512,768]{1,0:T(8,128)} %fusion.7, bf16[1,2048,768]{2,1,0:T(8,128)(2,1)} %all-gather.7.cloned.1.call-done, bf16[64,8,2048]{2,1,0:T(8,128)(2,1)S(1)} %all-to-all-done), kind=kOutput, calls=%fused_computation.37 | convolution fusion | flops 1616510976 | bytes 10747904 | tf_op jit(solution)/shard_map/dot_general | solution.py:13
  150.4 4.5 %fusion.31 = f32[2048,768]{1,0:T(8,128)} fusion(bf16[512,768]{1,0:T(8,128)(2,1)S(1)} %get-tuple-element.20, bf16[64,8,2048]{2,1,0:T(8,128)(2,1)S(1)} %all-to-all-done), kind=kOutput, calls=%fused_computation.31 | convolution fusion | flops 1610612736 | bytes 9175040 | tf_op jit(solution)/shard_map/dot_general | solution.py:13
  155.0 5.6 %fusion.29 = f32[2048,768]{1,0:T(8,128)} fusion(bf16[512,768]{1,0:T(8,128)(2,1)} %get-tuple-element.21, bf16[64,8,2048]{2,1,0:T(8,128)(2,1)S(1)} %all-to-all-done), kind=kOutput, calls=%fused_computation.29 | convolution fusion | flops 1610612736 | bytes 9175040 | tf_op jit(solution)/shard_map/dot_general | solution.py:13
  160.7 1.1 copy-done.4
  161.7 6.7 %fusion.26 = f32[768,2048]{1,0:T(8,128)} fusion(bf16[512,768]{1,0:T(8,128)(2,1)S(1)} %copy-done.4, bf16[64,8,2048]{2,1,0:T(8,128)(2,1)} %all-to-all-done.2), kind=kOutput, calls=%fused_computation.26 | convolution fusion | flops 1610612736 | bytes 9175040 | tf_op jit(solution)/shard_map/dot_general | solution.py:13
  168.4 5.1 %fusion.18 = bf16[64,8,2048]{2,1,0:T(8,128)(2,1)} fusion(bf16[512,768]{1,0:T(8,128)(2,1)S(1)} %copy-done.4, bf16[1,768,2048]{2,1,0:T(8,128)(2,1)} %all-gather.11.cloned.1.call-done), kind=kOutput, calls=%fused_computation.20 | convolution fusion | flops 1611661312 | bytes 6029312 | tf_op jit(solution)/shard_map/dot_general | solution.py:13
  173.6 10.7 %all-to-all-start.1 = ((bf16[64,8,2048]{2,1,0:T(8,128)(2,1)}), bf16[64,8,2048]{2,1,0:T(8,128)(2,1)S(1)}, u32[]{:S(2)}, u32[]{:S(2)}) async-start(bf16[64,8,2048]{2,1,0:T(8,128)(2,1)} %fusion.18), calls=%async_computation.1 | async-start | bytes 4194304 | tf_op jit(solution)/shard_map/all_to_all | solution.py:69
  184.2 4.1 %fusion.5 = f32[512,2048]{1,0:T(8,128)S(1)} fusion(bf16[512,768]{1,0:T(8,128)(2,1)} %get-tuple-element.21, bf16[1,2048,768]{2,1,0:T(8,128)(2,1)} %all-gather.9.cloned.1.call-done), kind=kOutput, calls=%fused_computation.11 | convolution fusion | flops 1610612736 | bytes 8126464 | tf_op jit(solution)/shard_map/dot_general | solution.py:13
  188.3 3.2 fusion.21
  191.5 44.0 %all-to-all-done.1 = bf16[64,8,2048]{2,1,0:T(8,128)(2,1)S(1)} async-done(((bf16[64,8,2048]{2,1,0:T(8,128)(2,1)}), bf16[64,8,2048]{2,1,0:T(8,128)(2,1)S(1)}, u32[]{:S(2)}, u32[]{:S(2)}) %all-to-all-start.1) | async-done | bytes 2097184 | tf_op jit(solution)/shard_map/all_to_all | solution.py:69
  235.5 6.0 %all-to-all-start.3 = ((bf16[64,8,2048]{2,1,0:T(8,128)(2,1)}), bf16[64,8,2048]{2,1,0:T(8,128)(2,1)}, u32[]{:S(2)}, u32[]{:S(2)}) async-start(bf16[64,8,2048]{2,1,0:T(8,128)(2,1)} %fusion.21), calls=%async_computation.3 | async-start | bytes 4194304 | tf_op jit(solution)/shard_map/all_to_all | solution.py:91
  242.4 1.4 gather_fusion.1
  243.8 48.9 %all-to-all-done.3 = bf16[64,8,2048]{2,1,0:T(8,128)(2,1)} async-done(((bf16[64,8,2048]{2,1,0:T(8,128)(2,1)}), bf16[64,8,2048]{2,1,0:T(8,128)(2,1)}, u32[]{:S(2)}, u32[]{:S(2)}) %all-to-all-start.3) | async-done | bytes 2097184 | tf_op jit(solution)/shard_map/all_to_all | solution.py:91
  292.6 4.3 %gather_fusion.3 = bf16[256,2048]{1,0:T(8,128)(2,1)S(1)} fusion(bf16[512,2048]{1,0:T(8,128)(2,1)} %bitcast.16, s32[1024]{0:T(1024)S(1)} %pad_clamp_fusion), kind=kCustom, calls=%fused_computation.3 | custom fusion | bytes 2098176 | tf_op jit(solution)/shard_map/gather | solution.py:96
  296.9 2.2 fusion.25
  299.8 1.4 bitcast_reduce_fusion
  301.1 2.4 convert_bitcast_fusion.2
  303.5 2.8 convert_bitcast_fusion.1
  306.4 52.9 %reduce-scatter.8.cloned.1.call-done = f32[768,512]{1,0:T(8,128)} async-done(((f32[768,2048]{1,0:T(8,128)}), f32[768,512]{1,0:T(8,128)}) %reduce-scatter.8.cloned.1.call-update) | async-done | bytes 1572880 | tf_op jit(solution)/shard_map/reduce_scatter | solution.py:86
  359.3 2.4 convert_bitcast_fusion
  (54 shorter events, 6.8 us)
Async XLA Ops:
  7.2 22.9 %copy-start = (bf16[32,2048]{1,0:T(8,128)(2,1)S(1)}, bf16[32,2048]{1,0:T(8,128)(2,1)}, u32[]{:S(2)}) copy-start(bf16[32,2048]{1,0:T(8,128)(2,1)} %param.7) | copy-start | bytes 393220
  7.2 4.7 %copy-start.2 = (bf16[32,2048]{1,0:T(8,128)(2,1)S(1)}, bf16[32,2048]{1,0:T(8,128)(2,1)}, u32[]{:S(2)}) copy-start(bf16[32,2048]{1,0:T(8,128)(2,1)} %param.10) | copy-start | bytes 393220
  7.2 79.3 %all-gather.11.cloned.1.call-start = ((), (), s32[]{:S(2)}) async-start(), calls=%async_computation.12 | async-start | bytes 3932160 | tf_op jit(solution)/shard_map/all_gather | solution.py:61
  7.9 129.6 %all-gather.9.cloned.1.call-start = ((), (), s32[]{:S(2)}) async-start(), calls=%async_computation.11 | async-start | bytes 3932160 | tf_op jit(solution)/shard_map/all_gather | solution.py:60
  16.1 64.3 %all-to-all-start.2 = ((bf16[64,8,2048]{2,1,0:T(8,128)(2,1)}), bf16[64,8,2048]{2,1,0:T(8,128)(2,1)}, u32[]{:S(2)}, u32[]{:S(2)}) async-start(bf16[64,8,2048]{2,1,0:T(8,128)(2,1)} %fusion), calls=%async_computation.2 | async-start | bytes 4194304 | tf_op jit(solution)/shard_map/all_to_all | solution.py:70
  29.3 114.8 %all-gather.7.cloned.1.call-start = ((), (), s32[]{:S(2)}) async-start(), calls=%async_computation.10 | async-start | bytes 3932160 | tf_op jit(solution)/shard_map/all_gather | solution.py:59
  80.5 57.1 %all-to-all-start = ((bf16[64,8,2048]{2,1,0:T(8,128)(2,1)}), bf16[64,8,2048]{2,1,0:T(8,128)(2,1)S(1)}, u32[]{:S(2)}, u32[]{:S(2)}) async-start(bf16[64,8,2048]{2,1,0:T(8,128)(2,1)} %bitcast_select_fusion), calls=%async_computation | async-start | bytes 4194304 | tf_op jit(solution)/shard_map/all_to_all | solution.py:63
  86.3 214.8 %reduce-scatter.4.cloned.1.call-start = ((), (), s32[]{:S(2)}) async-start(), calls=%async_computation.7 | async-start | bytes 7864320 | tf_op jit(solution)/shard_map/reduce_scatter | solution.py:80
  154.9 148.6 %reduce-scatter.6.cloned.1.call-start = ((), (), s32[]{:S(2)}) async-start(), calls=%async_computation.8 | async-start | bytes 7864320 | tf_op jit(solution)/shard_map/reduce_scatter | solution.py:83
  160.6 1.1 copy-start.4
  160.6 198.6 %reduce-scatter.8.cloned.1.call-start = ((), (), s32[]{:S(2)}) async-start(), calls=%async_computation.9 | async-start | bytes 7864320 | tf_op jit(solution)/shard_map/reduce_scatter | solution.py:86
  173.6 61.9 %all-to-all-start.1 = ((bf16[64,8,2048]{2,1,0:T(8,128)(2,1)}), bf16[64,8,2048]{2,1,0:T(8,128)(2,1)S(1)}, u32[]{:S(2)}, u32[]{:S(2)}) async-start(bf16[64,8,2048]{2,1,0:T(8,128)(2,1)} %fusion.18), calls=%async_computation.1 | async-start | bytes 4194304 | tf_op jit(solution)/shard_map/all_to_all | solution.py:69
  184.2 4.1 %copy-start.6 = (bf16[1,2048,768]{2,1,0:T(8,128)(2,1)S(1)}, bf16[1,2048,768]{2,1,0:T(8,128)(2,1)}, u32[]{:S(2)}) copy-start(bf16[1,2048,768]{2,1,0:T(8,128)(2,1)} %all-gather.7.cloned.1.call-done) | copy-start | bytes 9437188
  191.5 50.7 %copy-start.5 = (s32[32,8]{0,1:T(8,128)S(1)}, s32[32,8]{0,1:T(8,128)}, u32[]{:S(2)}) copy-start(s32[32,8]{0,1:T(8,128)} %param.8) | copy-start | bytes 3076
  235.5 57.2 %all-to-all-start.3 = ((bf16[64,8,2048]{2,1,0:T(8,128)(2,1)}), bf16[64,8,2048]{2,1,0:T(8,128)(2,1)}, u32[]{:S(2)}, u32[]{:S(2)}) async-start(bf16[64,8,2048]{2,1,0:T(8,128)(2,1)} %fusion.21), calls=%async_computation.3 | async-start | bytes 4194304 | tf_op jit(solution)/shard_map/all_to_all | solution.py:91
  292.6 4.3 %copy-start.3 = (f32[32,2048]{1,0:T(8,128)S(1)}, f32[32,2048]{1,0:T(8,128)}, u32[]{:S(2)}) copy-start(f32[32,2048]{1,0:T(8,128)} %convert_element_type.74) | copy-start | bytes 786436
  301.1 60.5 %copy-start.1 = (bf16[32,2048]{1,0:T(8,128)(2,1)S(1)}, bf16[32,2048]{1,0:T(8,128)(2,1)}, u32[]{:S(2)}) copy-start(bf16[32,2048]{1,0:T(8,128)(2,1)} %param.7) | copy-start | bytes 393220
Sparse Core Ops, SparseCore 0:
  9.8 45.8 all-gather.10
  57.6 42.3 all-gather.8
  101.8 42.3 all-gather.6
  155.0 66.7 reduce-scatter.3
  224.3 66.2 reduce-scatter.5
  293.0 66.2 reduce-scatter.7
where the time goes:
time: 369 us; the launch traced here: 368 us
  waiting for transfers between devices  241 us (65%)
  matrix products  45.8 us (12%)
  starting transfers between devices  36.1 us (10%)
  other arithmetic  16.4 us (4%)
  local copies, waits for them, and re-layouts  14.7 us (4%)
  between operations  14.3 us (4%)
    reduce_scatter x1, waiting for transfers between devices, body(): lax.psum_scatter(contract(hidden, arrived_grads, 0, 0), 'dp', scatter_dim...  52.9 us
    all_to_all x1, waiting for transfers between devices, body(): lax.all_to_all(grad_pair, 'expert', split_axis=0, concat_axis=0, tiled=True)  48.9 us
    all_to_all x1, waiting for transfers between devices, body(): lax.all_to_all(cotangent_slots, 'expert', split_axis=0, concat_axis=0, ti...  46.2 us
    dot_general x9, matrix products, contract(): lax.dot_general(left_side, right_side, (((left_dim,), (right_dim,)), ((),...  45.8 us
    all_to_all x1, waiting for transfers between devices, body(): lax.all_to_all(token_slots, 'expert', split_axis=0, concat_axis=0, tiled=...  45.4 us
    all_to_all x1, waiting for transfers between devices, body(): lax.all_to_all(expert_out, 'expert', split_axis=0, concat_axis=0, tiled=T...  44 us
    all_to_all x1, starting transfers between devices, body(): lax.all_to_all(cotangent_slots, 'expert', split_axis=0, concat_axis=0, ti...  13.2 us
    all_to_all x1, starting transfers between devices, body(): lax.all_to_all(expert_out, 'expert', split_axis=0, concat_axis=0, tiled=T...  10.7 us
  transfers between devices with their start and end apart: 10, of which 6 were waited for; matrix products, arithmetic and copies ran while one was open for 17% of the time, Pallas kernels for 0%

commit v1 on v0

v1 whole, which is shorter than its diff:
```python
import jax
import jax.numpy as jnp
import numpy as np
from jax import lax
from jax.experimental import pallas as pl
from jax.experimental.pallas import tpu as pltpu
from jax.sharding import PartitionSpec as P

BF = jnp.bfloat16
F32 = jnp.float32
SLOTS = 8
META = 128
XC_PLANES = [[x * 16 + z * 2 + c for x in range(4) for c in range(2)] for z in range(8)]


def dot(left_side, right_side, left_dim, right_dim, precision=None):
    return lax.dot_general(
        left_side,
        right_side,
        (((left_dim,), (right_dim,)), ((), ())),
        precision=precision,
        preferred_element_type=F32,
    )


def along_z(value, way, cores=(0, 1)):
    pairs = []
    for i in range(lax.axis_size("expert")):
        step = way if i % 2 == 0 else -way
        if i % 2 in cores:
            pairs.append((i, i // 16 * 16 + (i % 16 // 2 + step) % 8 * 2 + i % 2))
    return lax.ppermute(value, "expert", pairs)


def other_core(value):
    return lax.ppermute(value, "expert", [(i, i ^ 1) for i in range(lax.axis_size("expert"))])


def gather_z(mine, first):
    own = jnp.concatenate([mine, other_core(mine)], axis=0)
    one = along_z(own, 1)
    two = along_z(one, 1)
    three = along_z(two, 1)
    four = along_z(three, 1, (1,))
    return jnp.concatenate([jnp.where(first, own, four), one, two, three], axis=0)


def scatter_z(partial, first):
    rows = partial.shape[0] // 4

    def block(i):
        return partial[i * rows : (i + 1) * rows]

    moved = along_z(block(0).astype(BF), -1, (1,))
    for i in (3, 2, 1):
        moved = along_z((block(i) + moved.astype(F32)).astype(BF), -1)
    total = moved.astype(F32) + jnp.where(first, block(0), 0.0)
    half = rows // 2
    return total[:half] + other_core(total[half:].astype(BF)).astype(F32)


def swap_rows(value):
    return lax.all_to_all(value, "expert", 0, 0, axis_index_groups=XC_PLANES, tiled=True)


def copies(pairs, sems):
    started = [
        pltpu.make_async_copy(source, target, sems.at[i])
        for i, (source, target) in enumerate(pairs)
    ]
    for copy in started:
        copy.start()
    return started


def pack_kernel(gate, up, down, out):
    width = gate.shape[1]
    out[:, :width] = gate[...]
    out[:, width : 2 * width] = up[...]
    out[:, 2 * width :] = down[...].astype(F32).T.astype(BF)


def unpack_kernel(packed, gate, up, down):
    width = gate.shape[1]
    gate[...] = packed[:, :width]
    up[...] = packed[:, width : 2 * width]
    down[...] = packed[:, 2 * width :].astype(F32).T.astype(BF)


def expert_kernel(
    rows, weights, out, pre, sums, rows_v, gate_up_v, down_v, pre_v, hidden, sums_v, sems
):
    part, hidden_width = down_v.shape[1:]
    both = 2 * hidden_width
    pairs = []
    for j in range(4):
        pairs += [
            (rows.at[:, j * part : (j + 1) * part], rows_v.at[j]),
            (weights.at[j, :, :both], gate_up_v.at[j]),
        ]
    for j in range(4):
        pairs += [
            (rows.at[:, (4 + j) * part : (5 + j) * part], rows_v.at[4 + j]),
            (weights.at[j, :, both:], down_v.at[j]),
        ]
    moves = copies(pairs, sems)
    for j in range(4):
        moves[2 * j].wait()
        moves[2 * j + 1].wait()
        product = dot(rows_v[j], gate_up_v[j], 1, 0)
        pre_v[...] = product if j == 0 else pre_v[...] + product
    for move in moves[8:]:
        move.wait()
    step = 128
    for i in range(0, pre_v.shape[0], step):
        at = slice(i, i + step)
        gate_vals, up_vals = pre_v[at, :hidden_width], pre_v[at, hidden_width:]
        sig_vals = 1.0 / (1.0 + jnp.exp(-gate_vals))
        act_vals = gate_vals * sig_vals
        hidden[at] = (act_vals * up_vals).astype(BF)
        grad_hidden = sum(dot(rows_v[4 + j, at], down_v[j], 1, 0) for j in range(4))
        slope_vals = sig_vals * (1.0 + gate_vals * (1.0 - sig_vals))
        pre[at, :hidden_width] = (grad_hidden * up_vals * slope_vals).astype(BF)
        pre[at, hidden_width:] = (grad_hidden * act_vals).astype(BF)
    outs = []
    for j in range(4):
        sums_v[j, :, :both] = dot(rows_v[j], pre[...], 0, 0).astype(BF)
        sums_v[j, :, both:] = dot(rows_v[4 + j], hidden[...], 0, 0).astype(BF)
        outs.append(
            pltpu.make_async_copy(
                sums_v.at[j], sums.at[j * part : (j + 1) * part], sems.at[16 + j]
            )
        )
        outs[-1].start()
    for j in range(4):
        out[:, j * part : (j + 1) * part] = dot(hidden[...], down_v[j], 1, 1).astype(BF)
    for move in outs:
        move.wait()


def pair_kernel(pre, weights, out, gate_up_v, sems):
    part, gate_up = gate_up_v.shape[1:]
    moves = copies([(weights.at[j, :, :gate_up], gate_up_v.at[j]) for j in range(4)], sems)
    for j in range(4):
        moves[j].wait()
        out[:, j * part : (j + 1) * part] = dot(pre[...], gate_up_v[j], 1, 1).astype(BF)


ANY = pl.BlockSpec(memory_space=pl.ANY)
VMEM = pl.BlockSpec(memory_space=pltpu.VMEM)


def call(kernel, in_specs, out_specs, outs, scratch=(), sems=0):
    held = [pltpu.VMEM(*shape) for shape in scratch]
    return pl.pallas_call(
        kernel,
        in_specs=in_specs,
        out_specs=out_specs,
        out_shape=[jax.ShapeDtypeStruct(*out) for out in outs],
        scratch_shapes=held + [pltpu.SemaphoreType.DMA((sems,))] * (sems > 0),
        compiler_params=pltpu.CompilerParams(vmem_limit_bytes=44 * 2**20),
        cost_estimate=pl.CostEstimate(flops=1, transcendentals=0, bytes_accessed=1),
    )


def pack(gate, up, down):
    rows, width = gate.shape
    step = rows // 4
    return pl.pallas_call(
        pack_kernel,
        grid=(4,),
        in_specs=[
            pl.BlockSpec((step, width), lambda i: (i, 0)),
            pl.BlockSpec((step, width), lambda i: (i, 0)),
            pl.BlockSpec((width, step), lambda i: (0, i)),
        ],
        out_specs=pl.BlockSpec((step, 3 * width), lambda i: (i, 0)),
        out_shape=jax.ShapeDtypeStruct((rows, 3 * width), BF),
    )(gate, up, down)


def unpack(packed):
    rows, width = packed.shape[0], packed.shape[1] // 3
    step = rows // 4
    return pl.pallas_call(
        unpack_kernel,
        grid=(4,),
        in_specs=[pl.BlockSpec((step, 3 * width), lambda i: (i, 0))],
        out_specs=[
            pl.BlockSpec((step, width), lambda i: (i, 0)),
            pl.BlockSpec((step, width), lambda i: (i, 0)),
            pl.BlockSpec((width, step), lambda i: (0, i)),
        ],
        out_shape=[
            jax.ShapeDtypeStruct((rows, width), BF),
            jax.ShapeDtypeStruct((rows, width), BF),
            jax.ShapeDtypeStruct((width, rows), BF),
        ],
    )(packed)


def pieces(value):
    high = lax.reduce_precision(value, 8, 7)
    mid = lax.reduce_precision(value - high, 8, 7)
    return high, mid, value - high - mid


def body(tokens, expert_ids, gate_probs, grad_out, w_gate, w_up, w_down):
    me = lax.axis_index("expert")
    z, first = me % 16 // 2, me % 2 == 0
    rows, width = tokens.shape
    top = expert_ids.shape[1]
    hidden_width = w_gate.shape[2]
    part = width // 4
    count = 8
    held = count * rows

    experts = lax.all_gather(pack(w_gate[0], w_up[0], w_down[0]), "dp")

    meta = jnp.concatenate(
        [expert_ids.astype(F32), *pieces(gate_probs), jnp.zeros((rows, META - 4 * top), F32)],
        axis=1,
    ).astype(BF)
    sources = gather_z(jnp.concatenate([tokens, grad_out, meta], axis=1), first)
    meta = sources[:, 2 * width :].astype(F32)
    sources = sources[:, : 2 * width]

    group = jnp.arange(8, dtype=jnp.int32)
    dest = (group // 2 * 16 + z * 2 + group % 2).astype(F32)[None, :]
    match = [meta[:, k : k + 1] == dest for k in range(top)]
    probs = meta[:, top : 2 * top] + meta[:, 2 * top : 3 * top] + meta[:, 3 * top : 4 * top]
    holds = sum(hit.astype(F32) for hit in match)
    weight = sum(jnp.where(hit, probs[:, k : k + 1], 0.0) for k, hit in enumerate(match))
    token_id = np.arange(held)
    slot_id = np.arange(8 * count * SLOTS)
    earlier = (token_id[None, :] < token_id[:, None]) & (
        token_id[None, :] // rows == token_id[:, None] // rows
    )
    spread = jnp.asarray(slot_id[None, :] // (count * SLOTS) == np.arange(8)[:, None], F32)
    rank = dot(jnp.asarray(earlier, BF), holds.astype(BF), 1, 0)
    rank = dot(jnp.where(holds > 0, rank, -1.0).astype(BF), spread.astype(BF), 1, 0)
    wanted = np.where(
        slot_id[None, :] // SLOTS % count == token_id[:, None] // rows, slot_id[None, :] % SLOTS, -2
    )
    fills = rank == jnp.asarray(wanted, F32)
    select = fills.astype(BF)
    weights = jnp.where(fills, dot(weight, spread, 1, 0, lax.Precision.HIGHEST), 0.0)
    slot_weight = dot(weights, jnp.ones((held, 1), F32), 0, 0, lax.Precision.HIGHEST)

    scale = jnp.where(jnp.arange(2 * width)[None, :] < width, 1.0, slot_weight)
    arrived = swap_rows((dot(select, sources, 0, 0) * scale).astype(BF))

    slots = arrived.shape[0]
    wide = (slots, 2 * hidden_width)
    expert_out, grad_pre, sums = call(
        expert_kernel,
        [ANY] * 2,
        [VMEM, VMEM, ANY],
        [((slots, width), BF), (wide, BF), ((width, 3 * hidden_width), BF)],
        [
            ((8, slots, part), BF),
            ((4, part, 2 * hidden_width), BF),
            ((4, part, hidden_width), BF),
            (wide, F32),
            ((slots, hidden_width), BF),
            ((4, part, 3 * hidden_width), BF),
        ],
        20,
    )(arrived, experts)
    weight_grads = lax.psum_scatter(sums, "dp", scatter_dimension=0, tiled=True)
    back_out = swap_rows(expert_out)
    (grad_pair,) = call(
        pair_kernel,
        [VMEM, ANY],
        [VMEM],
        [((slots, width), BF)],
        [((4, part, 2 * hidden_width), BF)],
        4,
    )(grad_pre, experts)

    back_grads = swap_rows(grad_pair)
    weight_high, weight_mid, _ = pieces(weights)
    layer_part = dot(weight_high.astype(BF), back_out, 1, 0) + dot(
        weight_mid.astype(BF), back_out, 1, 0
    )
    products = jnp.where(fills, dot(sources[:, width:], back_out, 1, 1), 0.0)
    products = dot(products, spread, 1, 1, lax.Precision.HIGHEST)
    prob_part = jnp.concatenate(
        [jnp.sum(jnp.where(hit, products, 0.0), axis=1, keepdims=True) for hit in match], axis=1
    )
    prob_part = jnp.concatenate(
        [*pieces(prob_part), jnp.zeros((held, META - 3 * top), F32)], axis=1
    )
    layer_sum = scatter_z(jnp.concatenate([layer_part, prob_part], axis=1), first)
    grad_tokens = scatter_z(dot(select, back_grads, 1, 0), first).astype(BF)
    layer_out = layer_sum[:, :width].astype(BF)
    prob_sum = layer_sum[:, width:]
    grad_probs = prob_sum[:, :top] + prob_sum[:, top : 2 * top] + prob_sum[:, 2 * top : 3 * top]
    grad_gate, grad_up, grad_down = unpack(weight_grads)
    return layer_out, grad_tokens, grad_probs, grad_gate[None], grad_up[None], grad_down[None]


def solution(mesh):
    return jax.shard_map(
        body,
        mesh=mesh,
        in_specs=(
            P(("dp", "expert"), None),
            P(("dp", "expert"), None),
            P(("dp", "expert"), None),
            P(("dp", "expert"), None),
            P("expert", "dp", None),
            P("expert", "dp", None),
            P("expert", None, "dp"),
        ),
        out_specs=(
            P(("dp", "expert"), None),
            P(("dp", "expert"), None),
            P(("dp", "expert"), None),
            P("expert", "dp", None),
            P("expert", "dp", None),
            P("expert", None, "dp"),
        ),
        check_vma=False,
    )
```

time: 369 us -> 255 us (0.69)
  waiting for transfers between devices: 241 us -> 73.2 us
  blocking collectives: 0 us -> 84.3 us
  matrix products: 45.8 us -> 10.6 us
  Pallas kernels: 0 us -> 29.4 us
  other arithmetic: 16.4 us -> 2.87 us
  starting transfers between devices: 36.1 us -> 28.8 us
  local copies, waits for them, and re-layouts: 14.7 us -> 10.2 us
    all_to_all x4 -> x1, waiting for transfers between devices: 184 us -> 20.6 us  [swap_rows(): lax.all_to_all(value, 'expert', 0, 0, axis_index_groups=XC_PLANES, tiled=...]
    all_to_all x0 -> x2, blocking collectives: none -> 84.3 us  [swap_rows(): lax.all_to_all(value, 'expert', 0, 0, axis_index_groups=XC_PLANES, tiled=...]
    reduce_scatter x3 -> x1, waiting for transfers between devices: 52.9 us -> 0.01 us  [body(): weight_grads = lax.psum_scatter(sums, 'dp', scatter_dimension=0, tiled=True)]
    ppermute x0 -> x15, waiting for transfers between devices: none -> 52.5 us  [the longest x12 50.7 us: along_z(): return lax.ppermute(value, 'expert', pairs)]
    dot_general x9, matrix products: 45.8 us -> 10.6 us  [dot(): lax.dot_general(left_side, right_side, (((left_dim,), (right_dim,)), ((),...]
    all_to_all x4 -> x1, starting transfers between devices: 35.6 us -> 4.54 us  [swap_rows(): lax.all_to_all(value, 'expert', 0, 0, axis_index_groups=XC_PLANES, tiled=...]
    pallas_call x0 -> x4, Pallas kernels: none -> 29.4 us  [the longest x1 15.6 us: body(): call(expert_kernel, [ANY] * 2, [VMEM, VMEM, ANY], [((slots, width), BF),...]
    ppermute x0 -> x15, starting transfers between devices: none -> 24.2 us  [the longest x12 20.7 us: along_z(): return lax.ppermute(value, 'expert', pairs)]
  transfers between devices with their start and end apart: 10 -> 18, of which waited for: 6 -> 14; matrix products, arithmetic and copies ran while one was open for 17% -> 8% of each run, Pallas kernels for 0% -> 2%
where the time goes in v1:
time: 255 us; the launch traced here: 254 us
  blocking collectives  84.3 us (33%)
  waiting for transfers between devices  73.2 us (29%)
  Pallas kernels  29.4 us (12%)
  starting transfers between devices  28.8 us (11%)
  between operations  14.5 us (6%)
  matrix products  10.6 us (4%)
  local copies, waits for them, and re-layouts  10.2 us (4%)
  other arithmetic  2.87 us (1%)
    all_to_all x2, blocking collectives, swap_rows(): lax.all_to_all(value, 'expert', 0, 0, axis_index_groups=XC_PLANES, tiled=...  84.3 us
    ppermute x12, waiting for transfers between devices, along_z(): return lax.ppermute(value, 'expert', pairs)  50.7 us
    ppermute x12, starting transfers between devices, along_z(): return lax.ppermute(value, 'expert', pairs)  20.7 us
    all_to_all x1, waiting for transfers between devices, swap_rows(): lax.all_to_all(value, 'expert', 0, 0, axis_index_groups=XC_PLANES, tiled=...  20.6 us
    pallas_call x1, Pallas kernels, body(): call(expert_kernel, [ANY] * 2, [VMEM, VMEM, ANY], [((slots, width), BF),...  15.6 us
    dot_general x9, matrix products, dot(): lax.dot_general(left_side, right_side, (((left_dim,), (right_dim,)), ((),...  10.6 us
    pallas_call x1, Pallas kernels, body(): call(pair_kernel, [VMEM, ANY], [VMEM], [((slots, width), BF)], [((4, part...  5.69 us
  transfers between devices with their start and end apart: 18, of which 14 were waited for; matrix products, arithmetic and copies ran while one was open for 8% of the time, Pallas kernels for 2%

profile of v1, /device:TPU:1, one launch (start us, length us, event | category | flops | bytes accessed | tf_op | source)
XLA Modules:
  0.0 254.0 jit_solution(7144025361018029735)
XLA Ops:
  7.2 4.2 %shard_map.145 = bf16[512,2304]{1,0:T(8,128)(2,1)} custom-call(bf16[512,768]{1,0:T(8,128)(2,1)} %bitcast.43, bf16[512,768]{1,0:T(8,128)(2,1)} %bitcast.44, bf16[768,512]{1,0:T(8,128)(2,1)} %bitcast.45), custom_call_target="tpu_custom_call" | custom-call | tf_op jit(solution)/shard_map/pallas_call | solution.py:169
  12.6 3.3 %collective-permute-start = (bf16[32,4224]{1,0:T(8,128)(2,1)S(1)}, bf16[32,4224]{1,0:T(8,128)(2,1)S(1)}, u32[]{:S(2)}, u32[]{:S(2)}) collective-permute-start(bf16[32,4224]{1,0:T(8,128)(2,1)S(1)} %concatenate.18), channel_id=1, source_target_pairs={{0,1},{1,0},{2,3},{3,2},{4,5},{5,4},{6,7},{7,6},{8,9},{9,8},{10,11... | collective-permute-start | bytes 811016 | tf_op jit(solution)/shard_map/ppermute | solution.py:36
  17.1 3.9 %collective-permute-start.1 = (bf16[64,4224]{1,0:T(8,128)(2,1)S(1)}, bf16[64,4224]{1,0:T(8,128)(2,1)S(1)}, u32[]{:S(2)}, u32[]{:S(2)}) collective-permute-start(bf16[64,4224]{1,0:T(8,128)(2,1)S(1)} %pad_maximum_fusion.1), channel_id=1, source_target_pairs={{0,2},{1,15},{2,4},{3,1},{4,6},{5,3},{6,8},{7,5},{8,10},{9,7},{10,... | collective-permute-start | bytes 1622024 | tf_op jit(solution)/shard_map/ppermute | solution.py:32
  21.0 6.3 %collective-permute-done.1 = bf16[64,4224]{1,0:T(8,128)(2,1)S(1)} collective-permute-done((bf16[64,4224]{1,0:T(8,128)(2,1)S(1)}, bf16[64,4224]{1,0:T(8,128)(2,1)S(1)}, u32[]{:S(2)}, u32[]{:S(2)}) %collective-permute-start.1) | collective-permute-done | bytes 540704 | tf_op jit(solution)/shard_map/ppermute | solution.py:32
  27.3 3.1 %collective-permute-start.2 = (bf16[64,4224]{1,0:T(8,128)(2,1)S(1)}, bf16[64,4224]{1,0:T(8,128)(2,1)S(1)}, u32[]{:S(2)}, u32[]{:S(2)}) collective-permute-start(bf16[64,4224]{1,0:T(8,128)(2,1)S(1)} %collective-permute-done.1), channel_id=1, source_target_pairs={{0,2},{1,15},{2,4},{3,1},{4,6},{5,3},{6,8},{7,5},{8,10},{9,7},{10,... | collective-permute-start | bytes 1622024 | tf_op jit(solution)/shard_map/ppermute | solution.py:32
  30.4 6.3 %collective-permute-done.2 = bf16[64,4224]{1,0:T(8,128)(2,1)S(1)} collective-permute-done((bf16[64,4224]{1,0:T(8,128)(2,1)S(1)}, bf16[64,4224]{1,0:T(8,128)(2,1)S(1)}, u32[]{:S(2)}, u32[]{:S(2)}) %collective-permute-start.2) | collective-permute-done | bytes 540704 | tf_op jit(solution)/shard_map/ppermute | solution.py:32
  36.7 3.5 %collective-permute-start.3 = (bf16[64,4224]{1,0:T(8,128)(2,1)S(1)}, bf16[64,4224]{1,0:T(8,128)(2,1)S(1)}, u32[]{:S(2)}, u32[]{:S(2)}) collective-permute-start(bf16[64,4224]{1,0:T(8,128)(2,1)S(1)} %collective-permute-done.2), channel_id=1, source_target_pairs={{0,2},{1,15},{2,4},{3,1},{4,6},{5,3},{6,8},{7,5},{8,10},{9,7},{10,... | collective-permute-start | bytes 1622024 | tf_op jit(solution)/shard_map/ppermute | solution.py:32
  40.2 6.3 %collective-permute-done.3 = bf16[64,4224]{1,0:T(8,128)(2,1)S(1)} collective-permute-done((bf16[64,4224]{1,0:T(8,128)(2,1)S(1)}, bf16[64,4224]{1,0:T(8,128)(2,1)S(1)}, u32[]{:S(2)}, u32[]{:S(2)}) %collective-permute-start.3) | collective-permute-done | bytes 540704 | tf_op jit(solution)/shard_map/ppermute | solution.py:32
  46.6 5.4 %collective-permute-start.4 = (bf16[64,4224]{1,0:T(8,128)(2,1)S(1)}, bf16[64,4224]{1,0:T(8,128)(2,1)S(1)}, u32[]{:S(2)}, u32[]{:S(2)}) collective-permute-start(bf16[64,4224]{1,0:T(8,128)(2,1)S(1)} %collective-permute-done.3), channel_id=1, source_target_pairs={{1,15},{3,1},{5,3},{7,5},{9,7},{11,9},{13,11},{15,13},{17,31},{19,... | collective-permute-start | bytes 1622024 | tf_op jit(solution)/shard_map/ppermute | solution.py:32
  52.0 6.2 %collective-permute-done.4 = bf16[64,4224]{1,0:T(8,128)(2,1)S(1)} collective-permute-done((bf16[64,4224]{1,0:T(8,128)(2,1)S(1)}, bf16[64,4224]{1,0:T(8,128)(2,1)S(1)}, u32[]{:S(2)}, u32[]{:S(2)}) %collective-permute-start.4) | collective-permute-done | bytes 540704 | tf_op jit(solution)/shard_map/ppermute | solution.py:32
  61.6 1.3 multiply_convert_fusion
  62.9 53.6 %all_to_all.35 = bf16[8,64,4096]{2,1,0:T(8,128)(2,1)} all-to-all(bf16[8,64,4096]{2,1,0:T(8,128)(2,1)S(1)} %bitcast.42), channel_id=1, replica_groups={{0,1,16,17,32,33,48,49},{2,3,18,19,34,35,50,51},{4,5,20,21,36,37,52,53}..., dimensions={0} | all-to-all | bytes 8388608 | tf_op jit(solution)/shard_map/all_to_all | solution.py:63
  116.5 2.2 copy-done
  118.7 15.6 %shard_map.146 = (bf16[512,2048]{1,0:T(8,128)(2,1)}, bf16[512,1536]{1,0:T(8,128)(2,1)S(1)}, bf16[2048,2304]{1,0:T(8,128)(2,1)}) custom-call(bf16[512,4096]{1,0:T(8,128)(2,1)S(1)} %bitcast.34, bf16[4,512,2304]{2,1,0:T(8,128)(2,1)} %bitcast.36), custom_call_target="tpu_custom_call" | custom-call | flops 1 | bytes 1 | tf_op jit(solution)/shard_map/pallas_call | solution.py:255
  134.4 5.7 %shard_map.147 = bf16[512,2048]{1,0:T(8,128)(2,1)S(1)} custom-call(bf16[512,1536]{1,0:T(8,128)(2,1)S(1)} %get-tuple-element.13.pre, bf16[4,512,2304]{2,1,0:T(8,128)(2,1)} %bitcast.37), custom_call_target="tpu_custom_call" | custom-call | flops 1 | bytes 1 | tf_op jit(solution)/shard_map/pallas_call | solution.py:272
  140.1 30.7 %all_to_all.36 = bf16[8,64,2048]{2,1,0:T(8,128)(2,1)} all-to-all(bf16[8,64,2048]{2,1,0:T(8,128)(2,1)S(1)} %bitcast.35), channel_id=1, replica_groups={{0,1,16,17,32,33,48,49},{2,3,18,19,34,35,50,51},{4,5,20,21,36,37,52,53}..., dimensions={0} | all-to-all | bytes 4194304 | tf_op jit(solution)/shard_map/all_to_all | solution.py:63
  170.8 4.5 %all-to-all-start.1 = ((bf16[8,64,2048]{2,1,0:T(8,128)(2,1)}), bf16[8,64,2048]{2,1,0:T(8,128)(2,1)S(1)}, u32[]{:S(2)}, u32[]{:S(2)}) async-start(bf16[8,64,2048]{2,1,0:T(8,128)(2,1)} %bitcast.7), calls=%async_computation.1 | async-start | bytes 4194304 | tf_op jit(solution)/shard_map/all_to_all | solution.py:63
  175.3 2.4 fusion.98
  179.1 1.9 collective-permute-start.10
  181.0 20.6 %all-to-all-done.1 = bf16[8,64,2048]{2,1,0:T(8,128)(2,1)S(1)} async-done(((bf16[8,64,2048]{2,1,0:T(8,128)(2,1)}), bf16[8,64,2048]{2,1,0:T(8,128)(2,1)S(1)}, u32[]{:S(2)}, u32[]{:S(2)}) %all-to-all-start.1) | async-done | bytes 2097184 | tf_op jit(solution)/shard_map/all_to_all | solution.py:63
  201.7 1.9 convolution_select_fusion
  205.3 2.2 convolution_add_fusion
  207.5 2.6 %concatenate.22 = f32[256,2176]{1,0:T(8,128)S(1)} concatenate(f32[256,2048]{1,0:T(8,128)} %convolution_add_fusion, f32[256,8]{1,0:T(8,128)S(1)} %copy.42, f32[256,8]{1,0:T(8,128)S(1)} %copy.43, f32[256,8]{1,0:T(8,128)S(1)} %copy.44, f32[256,104]{1,0:T(8,128)S(1)} %broadcast_in_dim.188), dimensions={1} | concatenate | bytes 4456448 | tf_op jit(solution)/shard_map/concatenate | solution.py:294
  210.1 2.1 collective-permute-start.5
  213.7 6.3 %collective-permute-done.5 = bf16[64,2176]{1,0:T(8,128)(2,1)S(1)} collective-permute-done((bf16[64,2176]{1,0:T(8,128)(2,1)S(1)}, bf16[64,2176]{1,0:T(8,128)(2,1)S(1)}, u32[]{:S(2)}, u32[]{:S(2)}) %collective-permute-start.5) | collective-permute-done | bytes 278560 | tf_op jit(solution)/shard_map/ppermute | solution.py:32
  220.1 2.7 %collective-permute-done.11 = bf16[64,2048]{1,0:T(8,128)(2,1)S(1)} collective-permute-done((bf16[64,2048]{1,0:T(8,128)(2,1)S(1)}, bf16[64,2048]{1,0:T(8,128)(2,1)S(1)}, u32[]{:S(2)}, u32[]{:S(2)}) %collective-permute-start.11) | collective-permute-done | bytes 262176 | tf_op jit(solution)/shard_map/ppermute | solution.py:32
  222.9 3.8 %collective-permute-done.6 = bf16[64,2176]{1,0:T(8,128)(2,1)S(1)} collective-permute-done((bf16[64,2176]{1,0:T(8,128)(2,1)S(1)}, bf16[64,2176]{1,0:T(8,128)(2,1)S(1)}, u32[]{:S(2)}, u32[]{:S(2)}) %collective-permute-start.6) | collective-permute-done | bytes 278560 | tf_op jit(solution)/shard_map/ppermute | solution.py:32
  226.9 2.7 %collective-permute-done.12 = bf16[64,2048]{1,0:T(8,128)(2,1)S(1)} collective-permute-done((bf16[64,2048]{1,0:T(8,128)(2,1)S(1)}, bf16[64,2048]{1,0:T(8,128)(2,1)S(1)}, u32[]{:S(2)}, u32[]{:S(2)}) %collective-permute-start.12) | collective-permute-done | bytes 262176 | tf_op jit(solution)/shard_map/ppermute | solution.py:32
  229.7 3.8 %collective-permute-done.7 = bf16[64,2176]{1,0:T(8,128)(2,1)S(1)} collective-permute-done((bf16[64,2176]{1,0:T(8,128)(2,1)S(1)}, bf16[64,2176]{1,0:T(8,128)(2,1)S(1)}, u32[]{:S(2)}, u32[]{:S(2)}) %collective-permute-start.7) | collective-permute-done | bytes 278560 | tf_op jit(solution)/shard_map/ppermute | solution.py:32
  233.6 2.7 %collective-permute-done.13 = bf16[64,2048]{1,0:T(8,128)(2,1)S(1)} collective-permute-done((bf16[64,2048]{1,0:T(8,128)(2,1)S(1)}, bf16[64,2048]{1,0:T(8,128)(2,1)S(1)}, u32[]{:S(2)}, u32[]{:S(2)}) %collective-permute-start.13) | collective-permute-done | bytes 262176 | tf_op jit(solution)/shard_map/ppermute | solution.py:32
  236.5 3.8 %collective-permute-done.8 = bf16[64,2176]{1,0:T(8,128)(2,1)S(1)} collective-permute-done((bf16[64,2176]{1,0:T(8,128)(2,1)S(1)}, bf16[64,2176]{1,0:T(8,128)(2,1)S(1)}, u32[]{:S(2)}, u32[]{:S(2)}) %collective-permute-start.8) | collective-permute-done | bytes 278560 | tf_op jit(solution)/shard_map/ppermute | solution.py:32
  243.2 3.9 %shard_map.148 = (bf16[512,768]{1,0:T(8,128)(2,1)}, bf16[512,768]{1,0:T(8,128)(2,1)}, bf16[768,512]{1,0:T(8,128)(2,1)}) custom-call(bf16[512,2304]{1,0:T(8,128)(2,1)} %reduce-scatter.2.cloned.1.call-done.packed), custom_call_target="tpu_custom_call" | custom-call | tf_op jit(solution)/shard_map/pallas_call | solution.py:185
  (89 shorter events, 14.1 us)
Async XLA Ops:
  7.2 109.4 %all-gather.3.cloned.1.call-start = ((), (), s32[]{:S(2)}) async-start(), calls=%async_computation.5 | async-start | bytes 11796480 | tf_op jit(solution)/shard_map/all_gather | solution.py:218
  11.4 0.7 copy-start.10
  11.4 1.0 copy-start.9
  11.4 1.1 copy-start.6
  11.4 1.1 copy-start.7
  11.4 231.8 %reduce-scatter.2.cloned.1.call-start = ((), (), s32[]{:S(2)}) async-start(), calls=%async_computation.4 | async-start | bytes 11796480 | tf_op jit(solution)/shard_map/reduce_scatter | solution.py:270
  12.6 4.5 %collective-permute-start = (bf16[32,4224]{1,0:T(8,128)(2,1)S(1)}, bf16[32,4224]{1,0:T(8,128)(2,1)S(1)}, u32[]{:S(2)}, u32[]{:S(2)}) collective-permute-start(bf16[32,4224]{1,0:T(8,128)(2,1)S(1)} %concatenate.18), channel_id=1, source_target_pairs={{0,1},{1,0},{2,3},{3,2},{4,5},{5,4},{6,7},{7,6},{8,9},{9,8},{10,11... | collective-permute-start | bytes 811016 | tf_op jit(solution)/shard_map/ppermute | solution.py:36
  17.1 10.2 %collective-permute-start.1 = (bf16[64,4224]{1,0:T(8,128)(2,1)S(1)}, bf16[64,4224]{1,0:T(8,128)(2,1)S(1)}, u32[]{:S(2)}, u32[]{:S(2)}) collective-permute-start(bf16[64,4224]{1,0:T(8,128)(2,1)S(1)} %pad_maximum_fusion.1), channel_id=1, source_target_pairs={{0,2},{1,15},{2,4},{3,1},{4,6},{5,3},{6,8},{7,5},{8,10},{9,7},{10,... | collective-permute-start | bytes 1622024 | tf_op jit(solution)/shard_map/ppermute | solution.py:32
  27.3 34.2 %copy-start.3 = (bf16[64,4224]{1,0:T(8,128)(2,1)}, bf16[64,4224]{1,0:T(8,128)(2,1)S(1)}, u32[]{:S(2)}) copy-start(bf16[64,4224]{1,0:T(8,128)(2,1)S(1)} %collective-permute-done.1) | copy-start | bytes 1622020
  27.3 9.4 %collective-permute-start.2 = (bf16[64,4224]{1,0:T(8,128)(2,1)S(1)}, bf16[64,4224]{1,0:T(8,128)(2,1)S(1)}, u32[]{:S(2)}, u32[]{:S(2)}) collective-permute-start(bf16[64,4224]{1,0:T(8,128)(2,1)S(1)} %collective-permute-done.1), channel_id=1, source_target_pairs={{0,2},{1,15},{2,4},{3,1},{4,6},{5,3},{6,8},{7,5},{8,10},{9,7},{10,... | collective-permute-start | bytes 1622024 | tf_op jit(solution)/shard_map/ppermute | solution.py:32
  36.7 24.7 %copy-start.4 = (bf16[64,4224]{1,0:T(8,128)(2,1)}, bf16[64,4224]{1,0:T(8,128)(2,1)S(1)}, u32[]{:S(2)}) copy-start(bf16[64,4224]{1,0:T(8,128)(2,1)S(1)} %collective-permute-done.2) | copy-start | bytes 1622020
  36.7 9.8 %collective-permute-start.3 = (bf16[64,4224]{1,0:T(8,128)(2,1)S(1)}, bf16[64,4224]{1,0:T(8,128)(2,1)S(1)}, u32[]{:S(2)}, u32[]{:S(2)}) collective-permute-start(bf16[64,4224]{1,0:T(8,128)(2,1)S(1)} %collective-permute-done.2), channel_id=1, source_target_pairs={{0,2},{1,15},{2,4},{3,1},{4,6},{5,3},{6,8},{7,5},{8,10},{9,7},{10,... | collective-permute-start | bytes 1622024 | tf_op jit(solution)/shard_map/ppermute | solution.py:32
  46.5 14.9 %copy-start.5 = (bf16[64,4224]{1,0:T(8,128)(2,1)}, bf16[64,4224]{1,0:T(8,128)(2,1)S(1)}, u32[]{:S(2)}) copy-start(bf16[64,4224]{1,0:T(8,128)(2,1)S(1)} %collective-permute-done.3) | copy-start | bytes 1622020
  46.6 11.7 %collective-permute-start.4 = (bf16[64,4224]{1,0:T(8,128)(2,1)S(1)}, bf16[64,4224]{1,0:T(8,128)(2,1)S(1)}, u32[]{:S(2)}, u32[]{:S(2)}) collective-permute-start(bf16[64,4224]{1,0:T(8,128)(2,1)S(1)} %collective-permute-done.3), channel_id=1, source_target_pairs={{1,15},{3,1},{5,3},{7,5},{9,7},{11,9},{13,11},{15,13},{17,31},{19,... | collective-permute-start | bytes 1622024 | tf_op jit(solution)/shard_map/ppermute | solution.py:32
  58.4 1.4 copy-start.11
  58.4 1.4 copy-start.12
  58.4 1.4 copy-start.13
  58.5 1.9 copy-start.8
  116.5 2.2 copy-start
  170.8 30.9 %all-to-all-start.1 = ((bf16[8,64,2048]{2,1,0:T(8,128)(2,1)}), bf16[8,64,2048]{2,1,0:T(8,128)(2,1)S(1)}, u32[]{:S(2)}, u32[]{:S(2)}) async-start(bf16[8,64,2048]{2,1,0:T(8,128)(2,1)} %bitcast.7), calls=%async_computation.1 | async-start | bytes 4194304 | tf_op jit(solution)/shard_map/all_to_all | solution.py:63
  177.7 1.4 copy-start.1
  179.1 33.1 %collective-permute-start.10 = (bf16[64,2048]{1,0:T(8,128)(2,1)}, bf16[64,2048]{1,0:T(8,128)(2,1)}, u32[]{:S(2)}, u32[]{:S(2)}) collective-permute-start(bf16[64,2048]{1,0:T(8,128)(2,1)} %slice.256), channel_id=1, source_target_pairs={{1,3},{3,5},{5,7},{7,9},{9,11},{11,13},{13,15},{15,1},{17,19},{19,... | collective-permute-start | bytes 786440 | tf_op jit(solution)/shard_map/ppermute | solution.py:32
  210.1 12.7 %copy-start.2 = (f32[256,2048]{1,0:T(8,128)S(1)}, f32[256,2048]{1,0:T(8,128)}, u32[]{:S(2)}) copy-start(f32[256,2048]{1,0:T(8,128)} %copy-done.1) | copy-start | bytes 6291460
  210.1 9.9 %collective-permute-start.5 = (bf16[64,2176]{1,0:T(8,128)(2,1)S(1)}, bf16[64,2176]{1,0:T(8,128)(2,1)S(1)}, u32[]{:S(2)}, u32[]{:S(2)}) collective-permute-start(bf16[64,2176]{1,0:T(8,128)(2,1)S(1)} %slice.255), channel_id=1, source_target_pairs={{1,3},{3,5},{5,7},{7,9},{9,11},{11,13},{13,15},{15,1},{17,19},{19,... | collective-permute-start | bytes 835592 | tf_op jit(solution)/shard_map/ppermute | solution.py:32
  213.4 9.4 %collective-permute-start.11 = (bf16[64,2048]{1,0:T(8,128)(2,1)S(1)}, bf16[64,2048]{1,0:T(8,128)(2,1)S(1)}, u32[]{:S(2)}, u32[]{:S(2)}) collective-permute-start(bf16[64,2048]{1,0:T(8,128)(2,1)S(1)} %fusion.14), channel_id=1, source_target_pairs={{0,14},{1,3},{2,0},{3,5},{4,2},{5,7},{6,4},{7,9},{8,6},{9,11},{10,... | collective-permute-start | bytes 786440 | tf_op jit(solution)/shard_map/ppermute | solution.py:32
  220.0 6.7 %collective-permute-start.6 = (bf16[64,2176]{1,0:T(8,128)(2,1)S(1)}, bf16[64,2176]{1,0:T(8,128)(2,1)S(1)}, u32[]{:S(2)}, u32[]{:S(2)}) collective-permute-start(bf16[64,2176]{1,0:T(8,128)(2,1)S(1)} %fusion.9), channel_id=1, source_target_pairs={{0,14},{1,3},{2,0},{3,5},{4,2},{5,7},{6,4},{7,9},{8,6},{9,11},{10,... | collective-permute-start | bytes 835592 | tf_op jit(solution)/shard_map/ppermute | solution.py:32
  222.8 6.7 %collective-permute-start.12 = (bf16[64,2048]{1,0:T(8,128)(2,1)S(1)}, bf16[64,2048]{1,0:T(8,128)(2,1)S(1)}, u32[]{:S(2)}, u32[]{:S(2)}) collective-permute-start(bf16[64,2048]{1,0:T(8,128)(2,1)S(1)} %fusion.15), channel_id=1, source_target_pairs={{0,14},{1,3},{2,0},{3,5},{4,2},{5,7},{6,4},{7,9},{8,6},{9,11},{10,... | collective-permute-start | bytes 786440 | tf_op jit(solution)/shard_map/ppermute | solution.py:32
  226.8 6.7 %collective-permute-start.7 = (bf16[64,2176]{1,0:T(8,128)(2,1)S(1)}, bf16[64,2176]{1,0:T(8,128)(2,1)S(1)}, u32[]{:S(2)}, u32[]{:S(2)}) collective-permute-start(bf16[64,2176]{1,0:T(8,128)(2,1)S(1)} %fusion.10), channel_id=1, source_target_pairs={{0,14},{1,3},{2,0},{3,5},{4,2},{5,7},{6,4},{7,9},{8,6},{9,11},{10,... | collective-permute-start | bytes 835592 | tf_op jit(solution)/shard_map/ppermute | solution.py:32
  229.6 6.7 %collective-permute-start.13 = (bf16[64,2048]{1,0:T(8,128)(2,1)S(1)}, bf16[64,2048]{1,0:T(8,128)(2,1)S(1)}, u32[]{:S(2)}, u32[]{:S(2)}) collective-permute-start(bf16[64,2048]{1,0:T(8,128)(2,1)S(1)} %fusion.16), channel_id=1, source_target_pairs={{0,14},{1,3},{2,0},{3,5},{4,2},{5,7},{6,4},{7,9},{8,6},{9,11},{10,... | collective-permute-start | bytes 786440 | tf_op jit(solution)/shard_map/ppermute | solution.py:32
  233.5 6.7 %collective-permute-start.8 = (bf16[64,2176]{1,0:T(8,128)(2,1)S(1)}, bf16[64,2176]{1,0:T(8,128)(2,1)S(1)}, u32[]{:S(2)}, u32[]{:S(2)}) collective-permute-start(bf16[64,2176]{1,0:T(8,128)(2,1)S(1)} %fusion.11), channel_id=1, source_target_pairs={{0,14},{1,3},{2,0},{3,5},{4,2},{5,7},{6,4},{7,9},{8,6},{9,11},{10,... | collective-permute-start | bytes 835592 | tf_op jit(solution)/shard_map/ppermute | solution.py:32
  236.4 4.1 %collective-permute-start.14 = (bf16[32,2048]{1,0:T(8,128)(2,1)S(1)}, bf16[32,2048]{1,0:T(8,128)(2,1)S(1)}, u32[]{:S(2)}, u32[]{:S(2)}) collective-permute-start(bf16[32,2048]{1,0:T(8,128)(2,1)S(1)} %slice.258), channel_id=1, source_target_pairs={{0,1},{1,0},{2,3},{3,2},{4,5},{5,4},{6,7},{7,6},{8,9},{9,8},{10,11... | collective-permute-start | bytes 393224 | tf_op jit(solution)/shard_map/ppermute | solution.py:36
  240.3 1.4 collective-permute-start.9
Sparse Core Ops, SparseCore 0:
  11.5 98.4 all-gather.2
  134.5 89.4 reduce-scatter.1

commit v2 on v1

--- a/solution.py
+++ b/solution.py
@@ -77,18 +77,18 @@
     width = gate.shape[1]
     out[:, :width] = gate[...]
     out[:, width : 2 * width] = up[...]
-    out[:, 2 * width :] = down[...].astype(F32).T.astype(BF)
+    out[:, 2 * width :] = down[...].T
 
 
 def unpack_kernel(packed, gate, up, down):
     width = gate.shape[1]
     gate[...] = packed[:, :width]
     up[...] = packed[:, width : 2 * width]
-    down[...] = packed[:, 2 * width :].astype(F32).T.astype(BF)
+    down[...] = packed[:, 2 * width :].T
 
 
 def expert_kernel(
-    rows, weights, out, pre, sums, rows_v, gate_up_v, down_v, pre_v, hidden, sums_v, sems
+    rows, weights, out, pair, sums, rows_v, gate_up_v, down_v, pre_v, hidden, pre, sums_v, sems
 ):
     part, hidden_width = down_v.shape[1:]
     both = 2 * hidden_width
@@ -133,32 +133,40 @@
         )
         outs[-1].start()
     for j in range(4):
-        out[:, j * part : (j + 1) * part] = dot(hidden[...], down_v[j], 1, 1).astype(BF)
+        at = slice(j * part, (j + 1) * part)
+        pair[:, at] = dot(pre[...], gate_up_v[j], 1, 1).astype(BF)
+        out[:, at] = dot(hidden[...], down_v[j], 1, 1).astype(BF)
     for move in outs:
         move.wait()
 
 
-def pair_kernel(pre, weights, out, gate_up_v, sems):
-    part, gate_up = gate_up_v.shape[1:]
-    moves = copies([(weights.at[j, :, :gate_up], gate_up_v.at[j]) for j in range(4)], sems)
-    for j in range(4):
-        moves[j].wait()
-        out[:, j * part : (j + 1) * part] = dot(pre[...], gate_up_v[j], 1, 1).astype(BF)
+def combine_kernel(back, sources, weights, select, place, out, back_v, cot_v, sems):
+    width = back.shape[1]
+    moves = copies([(back, back_v), (sources.at[:, width : 2 * width], cot_v)], sems)
+    high = weights[...].astype(BF)
+    mid = (weights[...] - high.astype(F32)).astype(BF)
+    moves[0].wait()
+    out[:, :width] = dot(high, back_v[...], 1, 0) + dot(mid, back_v[...], 1, 0)
+    moves[1].wait()
+    products = dot(cot_v[...], back_v[...], 1, 1) * select[...].astype(F32)
+    group = dot(products, place[...], 1, 0, lax.Precision.HIGHEST)
+    high = group.astype(BF).astype(F32)
+    lane = lax.broadcasted_iota(jnp.int32, group.shape, 1)
+    out[:, width:] = jnp.where(lane < group.shape[1] // 2, high, group - high)
 
 
 ANY = pl.BlockSpec(memory_space=pl.ANY)
 VMEM = pl.BlockSpec(memory_space=pltpu.VMEM)
 
 
-def call(kernel, in_specs, out_specs, outs, scratch=(), sems=0):
-    held = [pltpu.VMEM(*shape) for shape in scratch]
+def call(kernel, in_specs, out_specs, outs, scratch, sems, limit):
     return pl.pallas_call(
         kernel,
         in_specs=in_specs,
         out_specs=out_specs,
         out_shape=[jax.ShapeDtypeStruct(*out) for out in outs],
-        scratch_shapes=held + [pltpu.SemaphoreType.DMA((sems,))] * (sems > 0),
-        compiler_params=pltpu.CompilerParams(vmem_limit_bytes=44 * 2**20),
+        scratch_shapes=[*(pltpu.VMEM(*held) for held in scratch), pltpu.SemaphoreType.DMA((sems,))],
+        compiler_params=pltpu.CompilerParams(vmem_limit_bytes=limit * 2**20),
         cost_estimate=pl.CostEstimate(flops=1, transcendentals=0, bytes_accessed=1),
     )
 
@@ -221,9 +229,9 @@
         [expert_ids.astype(F32), *pieces(gate_probs), jnp.zeros((rows, META - 4 * top), F32)],
         axis=1,
     ).astype(BF)
-    sources = gather_z(jnp.concatenate([tokens, grad_out, meta], axis=1), first)
-    meta = sources[:, 2 * width :].astype(F32)
-    sources = sources[:, : 2 * width]
+    gathered = gather_z(jnp.concatenate([tokens, grad_out, meta], axis=1), first)
+    meta = gathered[:, 2 * width :].astype(F32)
+    sources = gathered[:, : 2 * width]
 
     group = jnp.arange(8, dtype=jnp.int32)
     dest = (group // 2 * 16 + z * 2 + group % 2).astype(F32)[None, :]
@@ -252,50 +260,46 @@
 
     slots = arrived.shape[0]
     wide = (slots, 2 * hidden_width)
-    expert_out, grad_pre, sums = call(
+    expert_out, grad_pair, sums = call(
         expert_kernel,
         [ANY] * 2,
         [VMEM, VMEM, ANY],
-        [((slots, width), BF), (wide, BF), ((width, 3 * hidden_width), BF)],
+        [((slots, width), BF), ((slots, width), BF), ((width, 3 * hidden_width), BF)],
         [
             ((8, slots, part), BF),
             ((4, part, 2 * hidden_width), BF),
             ((4, part, hidden_width), BF),
             (wide, F32),
             ((slots, hidden_width), BF),
+            (wide, BF),
             ((4, part, 3 * hidden_width), BF),
         ],
         20,
+        56,
     )(arrived, experts)
     weight_grads = lax.psum_scatter(sums, "dp", scatter_dimension=0, tiled=True)
+
+    back_grads = swap_rows(grad_pair)
+    expert_out, back_grads = lax.optimization_barrier((expert_out, back_grads))
     back_out = swap_rows(expert_out)
-    (grad_pair,) = call(
-        pair_kernel,
-        [VMEM, ANY],
+    lane = jnp.arange(META, dtype=jnp.int32)[None, :] % (META // 2)
+    place = (lane == z * 8 + jnp.asarray(slot_id // (count * SLOTS), jnp.int32)[:, None]).astype(F32)
+    (layer_part,) = call(
+        combine_kernel,
+        [ANY, ANY, VMEM, VMEM, VMEM],
         [VMEM],
-        [((slots, width), BF)],
-        [((4, part, 2 * hidden_width), BF)],
-        4,
-    )(grad_pre, experts)
-
-    back_grads = swap_rows(grad_pair)
-    weight_high, weight_mid, _ = pieces(weights)
-    layer_part = dot(weight_high.astype(BF), back_out, 1, 0) + dot(
-        weight_mid.astype(BF), back_out, 1, 0
-    )
-    products = jnp.where(fills, dot(sources[:, width:], back_out, 1, 1), 0.0)
-    products = dot(products, spread, 1, 1, lax.Precision.HIGHEST)
-    prob_part = jnp.concatenate(
-        [jnp.sum(jnp.where(hit, products, 0.0), axis=1, keepdims=True) for hit in match], axis=1
-    )
-    prob_part = jnp.concatenate(
-        [*pieces(prob_part), jnp.zeros((held, META - 3 * top), F32)], axis=1
-    )
-    layer_sum = scatter_z(jnp.concatenate([layer_part, prob_part], axis=1), first)
+        [((held, width + META), F32)],
+        [((slots, width), BF), ((held, width), BF)],
+        2,
+        32,
+    )(back_out, gathered, weights, select, place)
+    layer_sum = scatter_z(layer_part, first)
     grad_tokens = scatter_z(dot(select, back_grads, 1, 0), first).astype(BF)
     layer_out = layer_sum[:, :width].astype(BF)
-    prob_sum = layer_sum[:, width:]
-    grad_probs = prob_sum[:, :top] + prob_sum[:, top : 2 * top] + prob_sum[:, 2 * top : 3 * top]
+    prob_sum = layer_sum[:, width : width + META // 2] + layer_sum[:, width + META // 2 :]
+    named = expert_ids % 16 // 2 * 8 + expert_ids // 16 * 2 + expert_ids % 2
+    named = named[:, :, None] == jnp.arange(META // 2, dtype=jnp.int32)
+    grad_probs = jnp.sum(jnp.where(named, prob_sum[:, None, :], 0.0), axis=2)
     grad_gate, grad_up, grad_down = unpack(weight_grads)
     return layer_out, grad_tokens, grad_probs, grad_gate[None], grad_up[None], grad_down[None]
 

time: 255 us -> 251 us (0.984)
  matrix products: 10.6 us -> 5.24 us
  local copies, waits for them, and re-layouts: 10.2 us -> 4.94 us
  Pallas kernels: 29.4 us -> 32.9 us
    dot_general x9 -> x5, matrix products: 10.6 us -> 5.24 us  [dot(): lax.dot_general(left_side, right_side, (((left_dim,), (right_dim,)), ((),...]
    pallas_call x1, Pallas kernels: 15.6 us -> 19.9 us  [body(): call(expert_kernel, [ANY] * 2, [VMEM, VMEM, ANY], [((slots, width), BF),...]
    concatenate x3 -> x1, local copies, waits for them, and re-layouts: 2.73 us -> 0.1 us  [body(): jnp.concatenate([tokens, grad_out, meta], axis=1)]
  transfers between devices with their start and end apart: 18 -> 18, of which waited for: 14 -> 14; matrix products, arithmetic and copies ran while one was open for 8% -> 5% of each run, Pallas kernels for 2% -> 2%
where the time goes in v2:
time: 251 us; the launch traced here: 250 us
  blocking collectives  85.4 us (34%)
  waiting for transfers between devices  73.7 us (29%)
  Pallas kernels  32.9 us (13%)
  starting transfers between devices  29.6 us (12%)
  between operations  14.5 us (6%)
  matrix products  5.24 us (2%)
  local copies, waits for them, and re-layouts  4.94 us (2%)
  other arithmetic  4.12 us (2%)
    all_to_all x2, blocking collectives, swap_rows(): lax.all_to_all(value, 'expert', 0, 0, axis_index_groups=XC_PLANES, tiled=...  85.4 us
    ppermute x12, waiting for transfers between devices, along_z(): return lax.ppermute(value, 'expert', pairs)  51.2 us
    all_to_all x1, waiting for transfers between devices, swap_rows(): lax.all_to_all(value, 'expert', 0, 0, axis_index_groups=XC_PLANES, tiled=...  20.6 us
    ppermute x12, starting transfers between devices, along_z(): return lax.ppermute(value, 'expert', pairs)  20.6 us
    pallas_call x1, Pallas kernels, body(): call(expert_kernel, [ANY] * 2, [VMEM, VMEM, ANY], [((slots, width), BF),...  19.9 us
    all_to_all x1, starting transfers between devices, swap_rows(): lax.all_to_all(value, 'expert', 0, 0, axis_index_groups=XC_PLANES, tiled=...  5.38 us
    dot_general x5, matrix products, dot(): lax.dot_general(left_side, right_side, (((left_dim,), (right_dim,)), ((),...  5.24 us
    pallas_call x1, Pallas kernels, body(): call(combine_kernel, [ANY, ANY, VMEM, VMEM, VMEM], [VMEM], [((held, width...  5.11 us
  transfers between devices with their start and end apart: 18, of which 14 were waited for; matrix products, arithmetic and copies ran while one was open for 5% of the time, Pallas kernels for 2%

profile of v2, /device:TPU:1, one launch (start us, length us, event | category | flops | bytes accessed | tf_op | source)
XLA Modules:
  0.0 250.4 jit_solution(8949008965345671385)
XLA Ops:
  7.2 4.1 %shard_map.154 = bf16[512,2304]{1,0:T(8,128)(2,1)} custom-call(bf16[512,768]{1,0:T(8,128)(2,1)} %bitcast.27, bf16[512,768]{1,0:T(8,128)(2,1)} %bitcast.28, bf16[768,512]{1,0:T(8,128)(2,1)} %bitcast.29), custom_call_target="tpu_custom_call" | custom-call | tf_op jit(solution)/shard_map/pallas_call | solution.py:177
  12.4 3.3 %collective-permute-start = (bf16[32,4224]{1,0:T(8,128)(2,1)S(1)}, bf16[32,4224]{1,0:T(8,128)(2,1)S(1)}, u32[]{:S(2)}, u32[]{:S(2)}) collective-permute-start(bf16[32,4224]{1,0:T(8,128)(2,1)S(1)} %concatenate.12), channel_id=1, source_target_pairs={{0,1},{1,0},{2,3},{3,2},{4,5},{5,4},{6,7},{7,6},{8,9},{9,8},{10,11... | collective-permute-start | bytes 811016 | tf_op jit(solution)/shard_map/ppermute | solution.py:36
  15.7 1.2 collective-permute-done
  16.9 3.9 %collective-permute-start.1 = (bf16[64,4224]{1,0:T(8,128)(2,1)S(1)}, bf16[64,4224]{1,0:T(8,128)(2,1)S(1)}, u32[]{:S(2)}, u32[]{:S(2)}) collective-permute-start(bf16[64,4224]{1,0:T(8,128)(2,1)S(1)} %pad_maximum_fusion.1), channel_id=1, source_target_pairs={{0,2},{1,15},{2,4},{3,1},{4,6},{5,3},{6,8},{7,5},{8,10},{9,7},{10,... | collective-permute-start | bytes 1622024 | tf_op jit(solution)/shard_map/ppermute | solution.py:32
  20.8 6.3 %collective-permute-done.1 = bf16[64,4224]{1,0:T(8,128)(2,1)S(1)} collective-permute-done((bf16[64,4224]{1,0:T(8,128)(2,1)S(1)}, bf16[64,4224]{1,0:T(8,128)(2,1)S(1)}, u32[]{:S(2)}, u32[]{:S(2)}) %collective-permute-start.1) | collective-permute-done | bytes 540704 | tf_op jit(solution)/shard_map/ppermute | solution.py:32
  27.1 3.1 %collective-permute-start.2 = (bf16[64,4224]{1,0:T(8,128)(2,1)S(1)}, bf16[64,4224]{1,0:T(8,128)(2,1)S(1)}, u32[]{:S(2)}, u32[]{:S(2)}) collective-permute-start(bf16[64,4224]{1,0:T(8,128)(2,1)S(1)} %collective-permute-done.1), channel_id=1, source_target_pairs={{0,2},{1,15},{2,4},{3,1},{4,6},{5,3},{6,8},{7,5},{8,10},{9,7},{10,... | collective-permute-start | bytes 1622024 | tf_op jit(solution)/shard_map/ppermute | solution.py:32
  30.3 6.3 %collective-permute-done.2 = bf16[64,4224]{1,0:T(8,128)(2,1)S(1)} collective-permute-done((bf16[64,4224]{1,0:T(8,128)(2,1)S(1)}, bf16[64,4224]{1,0:T(8,128)(2,1)S(1)}, u32[]{:S(2)}, u32[]{:S(2)}) %collective-permute-start.2) | collective-permute-done | bytes 540704 | tf_op jit(solution)/shard_map/ppermute | solution.py:32
  36.6 3.5 %collective-permute-start.3 = (bf16[64,4224]{1,0:T(8,128)(2,1)S(1)}, bf16[64,4224]{1,0:T(8,128)(2,1)S(1)}, u32[]{:S(2)}, u32[]{:S(2)}) collective-permute-start(bf16[64,4224]{1,0:T(8,128)(2,1)S(1)} %collective-permute-done.2), channel_id=1, source_target_pairs={{0,2},{1,15},{2,4},{3,1},{4,6},{5,3},{6,8},{7,5},{8,10},{9,7},{10,... | collective-permute-start | bytes 1622024 | tf_op jit(solution)/shard_map/ppermute | solution.py:32
  40.1 6.3 %collective-permute-done.3 = bf16[64,4224]{1,0:T(8,128)(2,1)S(1)} collective-permute-done((bf16[64,4224]{1,0:T(8,128)(2,1)S(1)}, bf16[64,4224]{1,0:T(8,128)(2,1)S(1)}, u32[]{:S(2)}, u32[]{:S(2)}) %collective-permute-start.3) | collective-permute-done | bytes 540704 | tf_op jit(solution)/shard_map/ppermute | solution.py:32
  46.4 5.4 %collective-permute-start.4 = (bf16[64,4224]{1,0:T(8,128)(2,1)S(1)}, bf16[64,4224]{1,0:T(8,128)(2,1)S(1)}, u32[]{:S(2)}, u32[]{:S(2)}) collective-permute-start(bf16[64,4224]{1,0:T(8,128)(2,1)S(1)} %collective-permute-done.3), channel_id=1, source_target_pairs={{1,15},{3,1},{5,3},{7,5},{9,7},{11,9},{13,11},{15,13},{17,31},{19,... | collective-permute-start | bytes 1622024 | tf_op jit(solution)/shard_map/ppermute | solution.py:32
  51.9 6.2 %collective-permute-done.4 = bf16[64,4224]{1,0:T(8,128)(2,1)S(1)} collective-permute-done((bf16[64,4224]{1,0:T(8,128)(2,1)S(1)}, bf16[64,4224]{1,0:T(8,128)(2,1)S(1)}, u32[]{:S(2)}, u32[]{:S(2)}) %collective-permute-start.4) | collective-permute-done | bytes 540704 | tf_op jit(solution)/shard_map/ppermute | solution.py:32
  58.2 1.2 pad_maximum_fusion.sources
  59.7 1.1 slice_reduce_fusion.7
  62.5 1.3 multiply_convert_fusion
  63.8 53.6 %all_to_all.34 = bf16[8,64,4096]{2,1,0:T(8,128)(2,1)} all-to-all(bf16[8,64,4096]{2,1,0:T(8,128)(2,1)S(1)} %bitcast.24), channel_id=1, replica_groups={{0,1,16,17,32,33,48,49},{2,3,18,19,34,35,50,51},{4,5,20,21,36,37,52,53}..., dimensions={0} | all-to-all | bytes 8388608 | tf_op jit(solution)/shard_map/all_to_all | solution.py:63
  117.4 19.9 %shard_map.155 = (bf16[512,2048]{1,0:T(8,128)(2,1)}, bf16[512,2048]{1,0:T(8,128)(2,1)}, bf16[2048,2304]{1,0:T(8,128)(2,1)}) custom-call(bf16[512,4096]{1,0:T(8,128)(2,1)} %bitcast.21, bf16[4,512,2304]{2,1,0:T(8,128)(2,1)} %bitcast.22), custom_call_target="tpu_custom_call" | custom-call | flops 1 | bytes 1 | tf_op jit(solution)/shard_map/pallas_call | solution.py:263
  137.4 31.8 %all_to_all.35 = bf16[8,64,2048]{2,1,0:T(8,128)(2,1)} all-to-all(bf16[8,64,2048]{2,1,0:T(8,128)(2,1)} %bitcast.26), channel_id=1, replica_groups={{0,1,16,17,32,33,48,49},{2,3,18,19,34,35,50,51},{4,5,20,21,36,37,52,53}..., dimensions={0} | all-to-all | bytes 4194304 | tf_op jit(solution)/shard_map/all_to_all | solution.py:63
  169.2 5.4 %all-to-all-start.2 = ((bf16[8,64,2048]{2,1,0:T(8,128)(2,1)}), bf16[8,64,2048]{2,1,0:T(8,128)(2,1)}, u32[]{:S(2)}, u32[]{:S(2)}) async-start(bf16[8,64,2048]{2,1,0:T(8,128)(2,1)} %bitcast.25), calls=%async_computation.2 | async-start | bytes 4194304 | tf_op jit(solution)/shard_map/all_to_all | solution.py:63
  174.6 2.3 fusion.90
  176.9 1.3 copy-done
  178.2 1.9 collective-permute-start.10
  180.4 20.6 %all-to-all-done.2 = bf16[8,64,2048]{2,1,0:T(8,128)(2,1)} async-done(((bf16[8,64,2048]{2,1,0:T(8,128)(2,1)}), bf16[8,64,2048]{2,1,0:T(8,128)(2,1)}, u32[]{:S(2)}, u32[]{:S(2)}) %all-to-all-start.2) | async-done | bytes 2097184 | tf_op jit(solution)/shard_map/all_to_all | solution.py:63
  201.0 5.1 %shard_map.156 = f32[256,2176]{1,0:T(8,128)S(1)} custom-call(bf16[512,2048]{1,0:T(8,128)(2,1)} %bitcast.10.back, bf16[256,4224]{1,0:T(8,128)(2,1)S(1)} %pad_maximum_fusion.sources, f32[256,512]{1,0:T(8,128)S(1)} %convolution_select_fusion.weights, bf16[256,512]{1,0:T(8,128)(2,1)S(1)} %get-tuple-element.55.select, f32[512,128]{1,0:T(8,128)S(1)} %compare_convert_fusion.place), custom_call_target="tpu_custom_call" | custom-call | flops 1 | bytes 1 | tf_op jit(solution)/shard_map/pallas_call | solution.py:287
  206.2 1.9 collective-permute-start.5
  209.5 6.4 %collective-permute-done.5 = bf16[64,2176]{1,0:T(8,128)(2,1)S(1)} collective-permute-done((bf16[64,2176]{1,0:T(8,128)(2,1)S(1)}, bf16[64,2176]{1,0:T(8,128)(2,1)S(1)}, u32[]{:S(2)}, u32[]{:S(2)}) %collective-permute-start.5) | collective-permute-done | bytes 278560 | tf_op jit(solution)/shard_map/ppermute | solution.py:32
  216.1 2.7 %collective-permute-done.11 = bf16[64,2048]{1,0:T(8,128)(2,1)S(1)} collective-permute-done((bf16[64,2048]{1,0:T(8,128)(2,1)S(1)}, bf16[64,2048]{1,0:T(8,128)(2,1)S(1)}, u32[]{:S(2)}, u32[]{:S(2)}) %collective-permute-start.11) | collective-permute-done | bytes 262176 | tf_op jit(solution)/shard_map/ppermute | solution.py:32
  218.9 4.2 %collective-permute-done.6 = bf16[64,2176]{1,0:T(8,128)(2,1)S(1)} collective-permute-done((bf16[64,2176]{1,0:T(8,128)(2,1)S(1)}, bf16[64,2176]{1,0:T(8,128)(2,1)S(1)}, u32[]{:S(2)}, u32[]{:S(2)}) %collective-permute-start.6) | collective-permute-done | bytes 278560 | tf_op jit(solution)/shard_map/ppermute | solution.py:32
  223.2 2.7 %collective-permute-done.12 = bf16[64,2048]{1,0:T(8,128)(2,1)S(1)} collective-permute-done((bf16[64,2048]{1,0:T(8,128)(2,1)S(1)}, bf16[64,2048]{1,0:T(8,128)(2,1)S(1)}, u32[]{:S(2)}, u32[]{:S(2)}) %collective-permute-start.12) | collective-permute-done | bytes 262176 | tf_op jit(solution)/shard_map/ppermute | solution.py:32
  226.0 3.8 %collective-permute-done.7 = bf16[64,2176]{1,0:T(8,128)(2,1)S(1)} collective-permute-done((bf16[64,2176]{1,0:T(8,128)(2,1)S(1)}, bf16[64,2176]{1,0:T(8,128)(2,1)S(1)}, u32[]{:S(2)}, u32[]{:S(2)}) %collective-permute-start.7) | collective-permute-done | bytes 278560 | tf_op jit(solution)/shard_map/ppermute | solution.py:32
  230.0 2.7 %collective-permute-done.13 = bf16[64,2048]{1,0:T(8,128)(2,1)S(1)} collective-permute-done((bf16[64,2048]{1,0:T(8,128)(2,1)S(1)}, bf16[64,2048]{1,0:T(8,128)(2,1)S(1)}, u32[]{:S(2)}, u32[]{:S(2)}) %collective-permute-start.13) | collective-permute-done | bytes 262176 | tf_op jit(solution)/shard_map/ppermute | solution.py:32
  232.8 3.7 %collective-permute-done.8 = bf16[64,2176]{1,0:T(8,128)(2,1)S(1)} collective-permute-done((bf16[64,2176]{1,0:T(8,128)(2,1)S(1)}, bf16[64,2176]{1,0:T(8,128)(2,1)S(1)}, u32[]{:S(2)}, u32[]{:S(2)}) %collective-permute-start.8) | collective-permute-done | bytes 278560 | tf_op jit(solution)/shard_map/ppermute | solution.py:32
  239.7 3.8 %shard_map.157 = (bf16[512,768]{1,0:T(8,128)(2,1)}, bf16[512,768]{1,0:T(8,128)(2,1)}, bf16[768,512]{1,0:T(8,128)(2,1)}) custom-call(bf16[512,2304]{1,0:T(8,128)(2,1)} %reduce-scatter.2.cloned.1.call-done.packed), custom_call_target="tpu_custom_call" | custom-call | tf_op jit(solution)/shard_map/pallas_call | solution.py:193
  (79 shorter events, 8.8 us)
Async XLA Ops:
  7.2 110.2 %all-gather.3.cloned.1.call-start = ((), (), s32[]{:S(2)}) async-start(), calls=%async_computation.5 | async-start | bytes 11796480 | tf_op jit(solution)/shard_map/all_gather | solution.py:226
  11.3 0.7 copy-start.6
  11.3 0.8 copy-start.7
  11.3 1.0 copy-start.3
  11.3 1.0 copy-start.4
  11.3 228.4 %reduce-scatter.2.cloned.1.call-start = ((), (), s32[]{:S(2)}) async-start(), calls=%async_computation.4 | async-start | bytes 11796480 | tf_op jit(solution)/shard_map/reduce_scatter | solution.py:280
  12.4 4.5 %collective-permute-start = (bf16[32,4224]{1,0:T(8,128)(2,1)S(1)}, bf16[32,4224]{1,0:T(8,128)(2,1)S(1)}, u32[]{:S(2)}, u32[]{:S(2)}) collective-permute-start(bf16[32,4224]{1,0:T(8,128)(2,1)S(1)} %concatenate.12), channel_id=1, source_target_pairs={{0,1},{1,0},{2,3},{3,2},{4,5},{5,4},{6,7},{7,6},{8,9},{9,8},{10,11... | collective-permute-start | bytes 811016 | tf_op jit(solution)/shard_map/ppermute | solution.py:36
  16.9 10.2 %collective-permute-start.1 = (bf16[64,4224]{1,0:T(8,128)(2,1)S(1)}, bf16[64,4224]{1,0:T(8,128)(2,1)S(1)}, u32[]{:S(2)}, u32[]{:S(2)}) collective-permute-start(bf16[64,4224]{1,0:T(8,128)(2,1)S(1)} %pad_maximum_fusion.1), channel_id=1, source_target_pairs={{0,2},{1,15},{2,4},{3,1},{4,6},{5,3},{6,8},{7,5},{8,10},{9,7},{10,... | collective-permute-start | bytes 1622024 | tf_op jit(solution)/shard_map/ppermute | solution.py:32
  27.1 9.4 %collective-permute-start.2 = (bf16[64,4224]{1,0:T(8,128)(2,1)S(1)}, bf16[64,4224]{1,0:T(8,128)(2,1)S(1)}, u32[]{:S(2)}, u32[]{:S(2)}) collective-permute-start(bf16[64,4224]{1,0:T(8,128)(2,1)S(1)} %collective-permute-done.1), channel_id=1, source_target_pairs={{0,2},{1,15},{2,4},{3,1},{4,6},{5,3},{6,8},{7,5},{8,10},{9,7},{10,... | collective-permute-start | bytes 1622024 | tf_op jit(solution)/shard_map/ppermute | solution.py:32
  36.6 9.8 %collective-permute-start.3 = (bf16[64,4224]{1,0:T(8,128)(2,1)S(1)}, bf16[64,4224]{1,0:T(8,128)(2,1)S(1)}, u32[]{:S(2)}, u32[]{:S(2)}) collective-permute-start(bf16[64,4224]{1,0:T(8,128)(2,1)S(1)} %collective-permute-done.2), channel_id=1, source_target_pairs={{0,2},{1,15},{2,4},{3,1},{4,6},{5,3},{6,8},{7,5},{8,10},{9,7},{10,... | collective-permute-start | bytes 1622024 | tf_op jit(solution)/shard_map/ppermute | solution.py:32
  46.4 11.7 %copy-start.2 = (bf16[64,4224]{1,0:T(8,128)(2,1)}, bf16[64,4224]{1,0:T(8,128)(2,1)S(1)}, u32[]{:S(2)}) copy-start(bf16[64,4224]{1,0:T(8,128)(2,1)S(1)} %collective-permute-done.3) | copy-start | bytes 1622020
  46.4 11.7 %collective-permute-start.4 = (bf16[64,4224]{1,0:T(8,128)(2,1)S(1)}, bf16[64,4224]{1,0:T(8,128)(2,1)S(1)}, u32[]{:S(2)}, u32[]{:S(2)}) collective-permute-start(bf16[64,4224]{1,0:T(8,128)(2,1)S(1)} %collective-permute-done.3), channel_id=1, source_target_pairs={{1,15},{3,1},{5,3},{7,5},{9,7},{11,9},{13,11},{15,13},{17,31},{19,... | collective-permute-start | bytes 1622024 | tf_op jit(solution)/shard_map/ppermute | solution.py:32
  59.4 1.4 copy-start.9
  59.4 1.4 copy-start.10
  59.5 1.4 copy-start.11
  59.5 1.9 copy-start.5
  169.2 5.4 %copy-start.8 = (s32[512]{0:T(512)S(1)}, s32[512]{0:T(512)}, u32[]{:S(2)}) copy-start(s32[512]{0:T(512)} %constant.134.clone) | copy-start | bytes 6148
  169.2 31.8 %all-to-all-start.2 = ((bf16[8,64,2048]{2,1,0:T(8,128)(2,1)}), bf16[8,64,2048]{2,1,0:T(8,128)(2,1)}, u32[]{:S(2)}, u32[]{:S(2)}) async-start(bf16[8,64,2048]{2,1,0:T(8,128)(2,1)} %bitcast.25), calls=%async_computation.2 | async-start | bytes 4194304 | tf_op jit(solution)/shard_map/all_to_all | solution.py:63
  176.9 1.3 copy-start
  178.2 29.9 %collective-permute-start.10 = (bf16[64,2048]{1,0:T(8,128)(2,1)S(1)}, bf16[64,2048]{1,0:T(8,128)(2,1)}, u32[]{:S(2)}, u32[]{:S(2)}) collective-permute-start(bf16[64,2048]{1,0:T(8,128)(2,1)S(1)} %slice.241), channel_id=1, source_target_pairs={{1,3},{3,5},{5,7},{7,9},{9,11},{11,13},{13,15},{15,1},{17,19},{19,... | collective-permute-start | bytes 786440 | tf_op jit(solution)/shard_map/ppermute | solution.py:32
  201.0 7.1 %copy-start.1 = (f32[256,2048]{1,0:T(8,128)S(1)}, f32[256,2048]{1,0:T(8,128)}, u32[]{:S(2)}) copy-start(f32[256,2048]{1,0:T(8,128)} %copy-done) | copy-start | bytes 6291460
  206.2 9.7 %collective-permute-start.5 = (bf16[64,2176]{1,0:T(8,128)(2,1)S(1)}, bf16[64,2176]{1,0:T(8,128)(2,1)S(1)}, u32[]{:S(2)}, u32[]{:S(2)}) collective-permute-start(bf16[64,2176]{1,0:T(8,128)(2,1)S(1)} %slice.240), channel_id=1, source_target_pairs={{1,3},{3,5},{5,7},{7,9},{9,11},{11,13},{13,15},{15,1},{17,19},{19,... | collective-permute-start | bytes 835592 | tf_op jit(solution)/shard_map/ppermute | solution.py:32
  209.2 9.6 %collective-permute-start.11 = (bf16[64,2048]{1,0:T(8,128)(2,1)S(1)}, bf16[64,2048]{1,0:T(8,128)(2,1)S(1)}, u32[]{:S(2)}, u32[]{:S(2)}) collective-permute-start(bf16[64,2048]{1,0:T(8,128)(2,1)S(1)} %fusion.5), channel_id=1, source_target_pairs={{0,14},{1,3},{2,0},{3,5},{4,2},{5,7},{6,4},{7,9},{8,6},{9,11},{10,... | collective-permute-start | bytes 786440 | tf_op jit(solution)/shard_map/ppermute | solution.py:32
  216.0 7.1 %collective-permute-start.6 = (bf16[64,2176]{1,0:T(8,128)(2,1)S(1)}, bf16[64,2176]{1,0:T(8,128)(2,1)S(1)}, u32[]{:S(2)}, u32[]{:S(2)}) collective-permute-start(bf16[64,2176]{1,0:T(8,128)(2,1)S(1)} %fusion.2), channel_id=1, source_target_pairs={{0,14},{1,3},{2,0},{3,5},{4,2},{5,7},{6,4},{7,9},{8,6},{9,11},{10,... | collective-permute-start | bytes 835592 | tf_op jit(solution)/shard_map/ppermute | solution.py:32
  218.8 7.1 %collective-permute-start.12 = (bf16[64,2048]{1,0:T(8,128)(2,1)S(1)}, bf16[64,2048]{1,0:T(8,128)(2,1)S(1)}, u32[]{:S(2)}, u32[]{:S(2)}) collective-permute-start(bf16[64,2048]{1,0:T(8,128)(2,1)S(1)} %fusion.6), channel_id=1, source_target_pairs={{0,14},{1,3},{2,0},{3,5},{4,2},{5,7},{6,4},{7,9},{8,6},{9,11},{10,... | collective-permute-start | bytes 786440 | tf_op jit(solution)/shard_map/ppermute | solution.py:32
  223.1 6.7 %collective-permute-start.7 = (bf16[64,2176]{1,0:T(8,128)(2,1)S(1)}, bf16[64,2176]{1,0:T(8,128)(2,1)S(1)}, u32[]{:S(2)}, u32[]{:S(2)}) collective-permute-start(bf16[64,2176]{1,0:T(8,128)(2,1)S(1)} %fusion.3), channel_id=1, source_target_pairs={{0,14},{1,3},{2,0},{3,5},{4,2},{5,7},{6,4},{7,9},{8,6},{9,11},{10,... | collective-permute-start | bytes 835592 | tf_op jit(solution)/shard_map/ppermute | solution.py:32
  225.9 6.7 %collective-permute-start.13 = (bf16[64,2048]{1,0:T(8,128)(2,1)S(1)}, bf16[64,2048]{1,0:T(8,128)(2,1)S(1)}, u32[]{:S(2)}, u32[]{:S(2)}) collective-permute-start(bf16[64,2048]{1,0:T(8,128)(2,1)S(1)} %fusion.7), channel_id=1, source_target_pairs={{0,14},{1,3},{2,0},{3,5},{4,2},{5,7},{6,4},{7,9},{8,6},{9,11},{10,... | collective-permute-start | bytes 786440 | tf_op jit(solution)/shard_map/ppermute | solution.py:32
  229.9 6.7 %collective-permute-start.8 = (bf16[64,2176]{1,0:T(8,128)(2,1)S(1)}, bf16[64,2176]{1,0:T(8,128)(2,1)S(1)}, u32[]{:S(2)}, u32[]{:S(2)}) collective-permute-start(bf16[64,2176]{1,0:T(8,128)(2,1)S(1)} %fusion.4), channel_id=1, source_target_pairs={{0,14},{1,3},{2,0},{3,5},{4,2},{5,7},{6,4},{7,9},{8,6},{9,11},{10,... | collective-permute-start | bytes 835592 | tf_op jit(solution)/shard_map/ppermute | solution.py:32
  232.7 4.0 %collective-permute-start.14 = (bf16[32,2048]{1,0:T(8,128)(2,1)S(1)}, bf16[32,2048]{1,0:T(8,128)(2,1)S(1)}, u32[]{:S(2)}, u32[]{:S(2)}) collective-permute-start(bf16[32,2048]{1,0:T(8,128)(2,1)S(1)} %slice.243), channel_id=1, source_target_pairs={{0,1},{1,0},{2,3},{3,2},{4,5},{5,4},{6,7},{7,6},{8,9},{9,8},{10,11... | collective-permute-start | bytes 393224 | tf_op jit(solution)/shard_map/ppermute | solution.py:36
  236.7 1.4 collective-permute-start.9
Sparse Core Ops, SparseCore 0:
  11.5 98.3 all-gather.2
  137.5 89.5 reduce-scatter.1

commit v3 on v2

--- a/solution.py
+++ b/solution.py
@@ -73,25 +73,38 @@
     return started
 
 
-def pack_kernel(gate, up, down, out):
-    width = gate.shape[1]
-    out[:, :width] = gate[...]
-    out[:, width : 2 * width] = up[...]
-    out[:, 2 * width :] = down[...].T
-
-
-def unpack_kernel(packed, gate, up, down):
-    width = gate.shape[1]
-    gate[...] = packed[:, :width]
-    up[...] = packed[:, width : 2 * width]
-    down[...] = packed[:, 2 * width :].T
+def pack_moves(gate, up, down, packed):
+    rows, width = gate.shape
+    rest = width - rows
+    at = 2 * width + rows
+    return [
+        (gate, packed.at[:, :width]),
+        (up, packed.at[:, width : 2 * width]),
+        (down.at[:rows], packed.at[:, 2 * width : at]),
+        (down.at[rows:, :rest], packed.at[:rest, at:]),
+        (down.at[rows:, rest:], packed.at[rest:, at:]),
+    ]
+
+
+def pack_kernel(gate, up, down, packed, sems):
+    for move in copies(pack_moves(gate, up, down, packed), sems):
+        move.wait()
+
+
+def unpack_kernel(packed, gate, up, down, sems):
+    moves = [(source, target) for target, source in pack_moves(gate, up, down, packed)]
+    for move in copies(moves, sems):
+        move.wait()
 
 
 def expert_kernel(
-    rows, weights, out, pair, sums, rows_v, gate_up_v, down_v, pre_v, hidden, pre, sums_v, sems
+    rows, weights, out, pair, sums, rows_v, gate_up_v, down_v, pre_v, grad_v, hidden, pre, sums_v,
+    out_v, pair_v, sems
 ):
-    part, hidden_width = down_v.shape[1:]
+    part, rest = down_v.shape[2], down_v.shape[1] - down_v.shape[2]
+    hidden_width = down_v.shape[1]
     both = 2 * hidden_width
+    last = both + part
     pairs = []
     for j in range(4):
         pairs += [
@@ -101,7 +114,9 @@
     for j in range(4):
         pairs += [
             (rows.at[:, (4 + j) * part : (5 + j) * part], rows_v.at[4 + j]),
-            (weights.at[j, :, both:], down_v.at[j]),
+            (weights.at[j, :, both:last], down_v.at[j, :part]),
+            (weights.at[j, :rest, last:], down_v.at[j, part:, :rest]),
+            (weights.at[j, rest:, last:], down_v.at[j, part:, rest:]),
         ]
     moves = copies(pairs, sems)
     for j in range(4):
@@ -109,8 +124,11 @@
         moves[2 * j + 1].wait()
         product = dot(rows_v[j], gate_up_v[j], 1, 0)
         pre_v[...] = product if j == 0 else pre_v[...] + product
-    for move in moves[8:]:
-        move.wait()
+    for j in range(4):
+        for move in moves[8 + 4 * j : 12 + 4 * j]:
+            move.wait()
+        product = dot(rows_v[4 + j], down_v[j], 1, 1)
+        grad_v[...] = product if j == 0 else grad_v[...] + product
     step = 128
     for i in range(0, pre_v.shape[0], step):
         at = slice(i, i + step)
@@ -118,24 +136,28 @@
         sig_vals = 1.0 / (1.0 + jnp.exp(-gate_vals))
         act_vals = gate_vals * sig_vals
         hidden[at] = (act_vals * up_vals).astype(BF)
-        grad_hidden = sum(dot(rows_v[4 + j, at], down_v[j], 1, 0) for j in range(4))
         slope_vals = sig_vals * (1.0 + gate_vals * (1.0 - sig_vals))
-        pre[at, :hidden_width] = (grad_hidden * up_vals * slope_vals).astype(BF)
-        pre[at, hidden_width:] = (grad_hidden * act_vals).astype(BF)
+        pre[at, :hidden_width] = (grad_v[at] * up_vals * slope_vals).astype(BF)
+        pre[at, hidden_width:] = (grad_v[at] * act_vals).astype(BF)
     outs = []
+
+    def leave(source, target):
+        outs.append(pltpu.make_async_copy(source, target, sems.at[len(moves) + len(outs)]))
+        outs[-1].start()
+
     for j in range(4):
         sums_v[j, :, :both] = dot(rows_v[j], pre[...], 0, 0).astype(BF)
-        sums_v[j, :, both:] = dot(rows_v[4 + j], hidden[...], 0, 0).astype(BF)
-        outs.append(
-            pltpu.make_async_copy(
-                sums_v.at[j], sums.at[j * part : (j + 1) * part], sems.at[16 + j]
-            )
-        )
-        outs[-1].start()
+        down_sum = dot(hidden[...], rows_v[4 + j], 0, 0).astype(BF)
+        sums_v[j, :, both:last] = down_sum[:part]
+        sums_v[j, :rest, last:] = down_sum[part:, :rest]
+        sums_v[j, rest:, last:] = down_sum[part:, rest:]
+        leave(sums_v.at[j], sums.at[j * part : (j + 1) * part])
     for j in range(4):
         at = slice(j * part, (j + 1) * part)
-        pair[:, at] = dot(pre[...], gate_up_v[j], 1, 1).astype(BF)
-        out[:, at] = dot(hidden[...], down_v[j], 1, 1).astype(BF)
+        pair_v[j] = dot(pre[...], gate_up_v[j], 1, 1).astype(BF)
+        leave(pair_v.at[j], pair.at[:, at])
+        out_v[j] = dot(hidden[...], down_v[j], 1, 0).astype(BF)
+        leave(out_v.at[j], out.at[:, at])
     for move in outs:
         move.wait()
 
@@ -173,38 +195,15 @@
 
 def pack(gate, up, down):
     rows, width = gate.shape
-    step = rows // 4
-    return pl.pallas_call(
-        pack_kernel,
-        grid=(4,),
-        in_specs=[
-            pl.BlockSpec((step, width), lambda i: (i, 0)),
-            pl.BlockSpec((step, width), lambda i: (i, 0)),
-            pl.BlockSpec((width, step), lambda i: (0, i)),
-        ],
-        out_specs=pl.BlockSpec((step, 3 * width), lambda i: (i, 0)),
-        out_shape=jax.ShapeDtypeStruct((rows, 3 * width), BF),
-    )(gate, up, down)
+    return call(pack_kernel, [ANY] * 3, [VMEM], [((rows, 3 * width), BF)], [], 5, 16)(
+        gate, up, down
+    )[0]
 
 
 def unpack(packed):
     rows, width = packed.shape[0], packed.shape[1] // 3
-    step = rows // 4
-    return pl.pallas_call(
-        unpack_kernel,
-        grid=(4,),
-        in_specs=[pl.BlockSpec((step, 3 * width), lambda i: (i, 0))],
-        out_specs=[
-            pl.BlockSpec((step, width), lambda i: (i, 0)),
-            pl.BlockSpec((step, width), lambda i: (i, 0)),
-            pl.BlockSpec((width, step), lambda i: (0, i)),
-        ],
-        out_shape=[
-            jax.ShapeDtypeStruct((rows, width), BF),
-            jax.ShapeDtypeStruct((rows, width), BF),
-            jax.ShapeDtypeStruct((width, rows), BF),
-        ],
-    )(packed)
+    outs = [((rows, width), BF), ((rows, width), BF), ((width, rows), BF)]
+    return call(unpack_kernel, [VMEM], [ANY] * 3, outs, [], 5, 16)(packed)
 
 
 def pieces(value):
@@ -263,18 +262,21 @@
     expert_out, grad_pair, sums = call(
         expert_kernel,
         [ANY] * 2,
-        [VMEM, VMEM, ANY],
+        [ANY, ANY, ANY],
         [((slots, width), BF), ((slots, width), BF), ((width, 3 * hidden_width), BF)],
         [
             ((8, slots, part), BF),
             ((4, part, 2 * hidden_width), BF),
-            ((4, part, hidden_width), BF),
+            ((4, hidden_width, part), BF),
             (wide, F32),
+            ((slots, hidden_width), F32),
             ((slots, hidden_width), BF),
             (wide, BF),
             ((4, part, 3 * hidden_width), BF),
+            ((4, slots, part), BF),
+            ((4, slots, part), BF),
         ],
-        20,
+        36,
         56,
     )(arrived, experts)
     weight_grads = lax.psum_scatter(sums, "dp", scatter_dimension=0, tiled=True)

time: 251 us -> 251 us (level)
  local copies, waits for them, and re-layouts: 4.94 us -> 9.98 us
  Pallas kernels: 32.9 us -> 28.1 us
    unnamed x26 -> x34, local copies, waits for them, and re-layouts: 2.69 us -> 7.73 us
    pallas_call x3, Pallas kernels: 27.8 us -> 22.9 us  [the longest x1 19.9 us: body(): call(expert_kernel, [ANY] * 2, [ANY, ANY, ANY], [((slots, width), BF), ((...]
where the time goes in v3:
time: 251 us
  blocking collectives  85.5 us (34%)
  waiting for transfers between devices  73.7 us (29%)
  starting transfers between devices  29.6 us (12%)
  Pallas kernels  28.1 us (11%)
  between operations  14.5 us (6%)
  local copies, waits for them, and re-layouts  9.98 us (4%)
  matrix products  5.23 us (2%)
  other arithmetic  4.12 us (2%)
    all_to_all x2, blocking collectives, swap_rows(): lax.all_to_all(value, 'expert', 0, 0, axis_index_groups=XC_PLANES, tiled=...  85.5 us
    ppermute x12, waiting for transfers between devices, along_z(): return lax.ppermute(value, 'expert', pairs)  51.2 us
    all_to_all x1, waiting for transfers between devices, swap_rows(): lax.all_to_all(value, 'expert', 0, 0, axis_index_groups=XC_PLANES, tiled=...  20.6 us
    ppermute x12, starting transfers between devices, along_z(): return lax.ppermute(value, 'expert', pairs)  20.6 us
    pallas_call x1, Pallas kernels, body(): call(expert_kernel, [ANY] * 2, [ANY, ANY, ANY], [((slots, width), BF), ((...  19.9 us
    unnamed x34, local copies, waits for them, and re-layouts  7.73 us
    all_to_all x1, starting transfers between devices, swap_rows(): lax.all_to_all(value, 'expert', 0, 0, axis_index_groups=XC_PLANES, tiled=...  5.38 us
    dot_general x5, matrix products, dot(): lax.dot_general(left_side, right_side, (((left_dim,), (right_dim,)), ((),...  5.23 us
  transfers between devices with their start and end apart: 18, of which 14 were waited for; matrix products, arithmetic and copies ran while one was open for 5% of the time, Pallas kernels for 2%

profile of v3, /device:TPU:1, one launch (start us, length us, event | category | flops | bytes accessed | tf_op | source)
XLA Modules:
  0.0 250.6 jit_solution(4173180239934480496)
XLA Ops:
  10.6 1.6 shard_map.154
  13.4 3.3 %collective-permute-start = (bf16[32,4224]{1,0:T(8,128)(2,1)S(1)}, bf16[32,4224]{1,0:T(8,128)(2,1)S(1)}, u32[]{:S(2)}, u32[]{:S(2)}) collective-permute-start(bf16[32,4224]{1,0:T(8,128)(2,1)S(1)} %concatenate.12), channel_id=1, source_target_pairs={{0,1},{1,0},{2,3},{3,2},{4,5},{5,4},{6,7},{7,6},{8,9},{9,8},{10,11... | collective-permute-start | bytes 811016 | tf_op jit(solution)/shard_map/ppermute | solution.py:36
  16.7 1.2 collective-permute-done
  17.9 3.9 %collective-permute-start.1 = (bf16[64,4224]{1,0:T(8,128)(2,1)S(1)}, bf16[64,4224]{1,0:T(8,128)(2,1)S(1)}, u32[]{:S(2)}, u32[]{:S(2)}) collective-permute-start(bf16[64,4224]{1,0:T(8,128)(2,1)S(1)} %pad_maximum_fusion.1), channel_id=1, source_target_pairs={{0,2},{1,15},{2,4},{3,1},{4,6},{5,3},{6,8},{7,5},{8,10},{9,7},{10,... | collective-permute-start | bytes 1622024 | tf_op jit(solution)/shard_map/ppermute | solution.py:32
  21.8 6.3 %collective-permute-done.1 = bf16[64,4224]{1,0:T(8,128)(2,1)S(1)} collective-permute-done((bf16[64,4224]{1,0:T(8,128)(2,1)S(1)}, bf16[64,4224]{1,0:T(8,128)(2,1)S(1)}, u32[]{:S(2)}, u32[]{:S(2)}) %collective-permute-start.1) | collective-permute-done | bytes 540704 | tf_op jit(solution)/shard_map/ppermute | solution.py:32
  28.1 3.1 %collective-permute-start.2 = (bf16[64,4224]{1,0:T(8,128)(2,1)S(1)}, bf16[64,4224]{1,0:T(8,128)(2,1)S(1)}, u32[]{:S(2)}, u32[]{:S(2)}) collective-permute-start(bf16[64,4224]{1,0:T(8,128)(2,1)S(1)} %collective-permute-done.1), channel_id=1, source_target_pairs={{0,2},{1,15},{2,4},{3,1},{4,6},{5,3},{6,8},{7,5},{8,10},{9,7},{10,... | collective-permute-start | bytes 1622024 | tf_op jit(solution)/shard_map/ppermute | solution.py:32
  31.2 6.3 %collective-permute-done.2 = bf16[64,4224]{1,0:T(8,128)(2,1)S(1)} collective-permute-done((bf16[64,4224]{1,0:T(8,128)(2,1)S(1)}, bf16[64,4224]{1,0:T(8,128)(2,1)S(1)}, u32[]{:S(2)}, u32[]{:S(2)}) %collective-permute-start.2) | collective-permute-done | bytes 540704 | tf_op jit(solution)/shard_map/ppermute | solution.py:32
  37.5 3.5 %collective-permute-start.3 = (bf16[64,4224]{1,0:T(8,128)(2,1)S(1)}, bf16[64,4224]{1,0:T(8,128)(2,1)S(1)}, u32[]{:S(2)}, u32[]{:S(2)}) collective-permute-start(bf16[64,4224]{1,0:T(8,128)(2,1)S(1)} %collective-permute-done.2), channel_id=1, source_target_pairs={{0,2},{1,15},{2,4},{3,1},{4,6},{5,3},{6,8},{7,5},{8,10},{9,7},{10,... | collective-permute-start | bytes 1622024 | tf_op jit(solution)/shard_map/ppermute | solution.py:32
  41.0 6.3 %collective-permute-done.3 = bf16[64,4224]{1,0:T(8,128)(2,1)S(1)} collective-permute-done((bf16[64,4224]{1,0:T(8,128)(2,1)S(1)}, bf16[64,4224]{1,0:T(8,128)(2,1)S(1)}, u32[]{:S(2)}, u32[]{:S(2)}) %collective-permute-start.3) | collective-permute-done | bytes 540704 | tf_op jit(solution)/shard_map/ppermute | solution.py:32
  47.4 5.4 %collective-permute-start.4 = (bf16[64,4224]{1,0:T(8,128)(2,1)S(1)}, bf16[64,4224]{1,0:T(8,128)(2,1)S(1)}, u32[]{:S(2)}, u32[]{:S(2)}) collective-permute-start(bf16[64,4224]{1,0:T(8,128)(2,1)S(1)} %collective-permute-done.3), channel_id=1, source_target_pairs={{1,15},{3,1},{5,3},{7,5},{9,7},{11,9},{13,11},{15,13},{17,31},{19,... | collective-permute-start | bytes 1622024 | tf_op jit(solution)/shard_map/ppermute | solution.py:32
  52.8 6.2 %collective-permute-done.4 = bf16[64,4224]{1,0:T(8,128)(2,1)S(1)} collective-permute-done((bf16[64,4224]{1,0:T(8,128)(2,1)S(1)}, bf16[64,4224]{1,0:T(8,128)(2,1)S(1)}, u32[]{:S(2)}, u32[]{:S(2)}) %collective-permute-start.4) | collective-permute-done | bytes 540704 | tf_op jit(solution)/shard_map/ppermute | solution.py:32
  59.2 1.2 pad_maximum_fusion.sources
  63.5 1.3 multiply_convert_fusion
  64.8 53.6 %all_to_all.34 = bf16[8,64,4096]{2,1,0:T(8,128)(2,1)} all-to-all(bf16[8,64,4096]{2,1,0:T(8,128)(2,1)S(1)} %bitcast.27), channel_id=1, replica_groups={{0,1,16,17,32,33,48,49},{2,3,18,19,34,35,50,51},{4,5,20,21,36,37,52,53}..., dimensions={0} | all-to-all | bytes 8388608 | tf_op jit(solution)/shard_map/all_to_all | solution.py:63
  118.4 19.9 %shard_map.155 = (bf16[512,2048]{1,0:T(8,128)(2,1)}, bf16[512,2048]{1,0:T(8,128)(2,1)}, bf16[2048,2304]{1,0:T(8,128)(2,1)}) custom-call(bf16[512,4096]{1,0:T(8,128)(2,1)} %bitcast.24, bf16[4,512,2304]{2,1,0:T(8,128)(2,1)} %bitcast.25), custom_call_target="tpu_custom_call" | custom-call | flops 1 | bytes 1 | tf_op jit(solution)/shard_map/pallas_call | solution.py:262
  138.3 31.8 %all_to_all.35 = bf16[8,64,2048]{2,1,0:T(8,128)(2,1)} all-to-all(bf16[8,64,2048]{2,1,0:T(8,128)(2,1)} %bitcast.29), channel_id=1, replica_groups={{0,1,16,17,32,33,48,49},{2,3,18,19,34,35,50,51},{4,5,20,21,36,37,52,53}..., dimensions={0} | all-to-all | bytes 4194304 | tf_op jit(solution)/shard_map/all_to_all | solution.py:63
  170.1 5.4 %all-to-all-start.2 = ((bf16[8,64,2048]{2,1,0:T(8,128)(2,1)}), bf16[8,64,2048]{2,1,0:T(8,128)(2,1)}, u32[]{:S(2)}, u32[]{:S(2)}) async-start(bf16[8,64,2048]{2,1,0:T(8,128)(2,1)} %bitcast.28), calls=%async_computation.2 | async-start | bytes 4194304 | tf_op jit(solution)/shard_map/all_to_all | solution.py:63
  175.5 2.3 fusion.90
  177.9 1.3 copy-done.4
  179.2 1.9 collective-permute-start.10
  181.3 20.6 %all-to-all-done.2 = bf16[8,64,2048]{2,1,0:T(8,128)(2,1)} async-done(((bf16[8,64,2048]{2,1,0:T(8,128)(2,1)}), bf16[8,64,2048]{2,1,0:T(8,128)(2,1)}, u32[]{:S(2)}, u32[]{:S(2)}) %all-to-all-start.2) | async-done | bytes 2097184 | tf_op jit(solution)/shard_map/all_to_all | solution.py:63
  202.0 5.1 %shard_map.156 = f32[256,2176]{1,0:T(8,128)S(1)} custom-call(bf16[512,2048]{1,0:T(8,128)(2,1)} %bitcast.10.back, bf16[256,4224]{1,0:T(8,128)(2,1)S(1)} %pad_maximum_fusion.sources, f32[256,512]{1,0:T(8,128)S(1)} %convolution_select_fusion.weights, bf16[256,512]{1,0:T(8,128)(2,1)S(1)} %get-tuple-element.55.select, f32[512,128]{1,0:T(8,128)S(1)} %compare_convert_fusion.place), custom_call_target="tpu_custom_call" | custom-call | flops 1 | bytes 1 | tf_op jit(solution)/shard_map/pallas_call | solution.py:289
  207.1 1.9 collective-permute-start.5
  210.5 6.4 %collective-permute-done.5 = bf16[64,2176]{1,0:T(8,128)(2,1)S(1)} collective-permute-done((bf16[64,2176]{1,0:T(8,128)(2,1)S(1)}, bf16[64,2176]{1,0:T(8,128)(2,1)S(1)}, u32[]{:S(2)}, u32[]{:S(2)}) %collective-permute-start.5) | collective-permute-done | bytes 278560 | tf_op jit(solution)/shard_map/ppermute | solution.py:32
  217.0 2.7 %collective-permute-done.11 = bf16[64,2048]{1,0:T(8,128)(2,1)S(1)} collective-permute-done((bf16[64,2048]{1,0:T(8,128)(2,1)S(1)}, bf16[64,2048]{1,0:T(8,128)(2,1)S(1)}, u32[]{:S(2)}, u32[]{:S(2)}) %collective-permute-start.11) | collective-permute-done | bytes 262176 | tf_op jit(solution)/shard_map/ppermute | solution.py:32
  219.8 4.2 %collective-permute-done.6 = bf16[64,2176]{1,0:T(8,128)(2,1)S(1)} collective-permute-done((bf16[64,2176]{1,0:T(8,128)(2,1)S(1)}, bf16[64,2176]{1,0:T(8,128)(2,1)S(1)}, u32[]{:S(2)}, u32[]{:S(2)}) %collective-permute-start.6) | collective-permute-done | bytes 278560 | tf_op jit(solution)/shard_map/ppermute | solution.py:32
  224.1 2.7 %collective-permute-done.12 = bf16[64,2048]{1,0:T(8,128)(2,1)S(1)} collective-permute-done((bf16[64,2048]{1,0:T(8,128)(2,1)S(1)}, bf16[64,2048]{1,0:T(8,128)(2,1)S(1)}, u32[]{:S(2)}, u32[]{:S(2)}) %collective-permute-start.12) | collective-permute-done | bytes 262176 | tf_op jit(solution)/shard_map/ppermute | solution.py:32
  227.0 3.8 %collective-permute-done.7 = bf16[64,2176]{1,0:T(8,128)(2,1)S(1)} collective-permute-done((bf16[64,2176]{1,0:T(8,128)(2,1)S(1)}, bf16[64,2176]{1,0:T(8,128)(2,1)S(1)}, u32[]{:S(2)}, u32[]{:S(2)}) %collective-permute-start.7) | collective-permute-done | bytes 278560 | tf_op jit(solution)/shard_map/ppermute | solution.py:32
  230.9 2.7 %collective-permute-done.13 = bf16[64,2048]{1,0:T(8,128)(2,1)S(1)} collective-permute-done((bf16[64,2048]{1,0:T(8,128)(2,1)S(1)}, bf16[64,2048]{1,0:T(8,128)(2,1)S(1)}, u32[]{:S(2)}, u32[]{:S(2)}) %collective-permute-start.13) | collective-permute-done | bytes 262176 | tf_op jit(solution)/shard_map/ppermute | solution.py:32
  233.7 3.7 %collective-permute-done.8 = bf16[64,2176]{1,0:T(8,128)(2,1)S(1)} collective-permute-done((bf16[64,2176]{1,0:T(8,128)(2,1)S(1)}, bf16[64,2176]{1,0:T(8,128)(2,1)S(1)}, u32[]{:S(2)}, u32[]{:S(2)}) %collective-permute-start.8) | collective-permute-done | bytes 278560 | tf_op jit(solution)/shard_map/ppermute | solution.py:32
  240.7 1.7 copy-done
  242.3 1.4 shard_map.157
  (87 shorter events, 13.3 us)
Async XLA Ops:
  7.2 111.2 %all-gather.3.cloned.1.call-start = ((), (), s32[]{:S(2)}) async-start(), calls=%async_computation.5 | async-start | bytes 11796480 | tf_op jit(solution)/shard_map/all_gather | solution.py:225
  7.2 1.1 copy-start.1
  8.3 1.1 copy-start.2
  9.5 1.1 copy-start.3
  12.3 1.0 copy-start.7
  12.3 1.0 copy-start.8
  12.3 228.3 %reduce-scatter.2.cloned.1.call-start = ((), (), s32[]{:S(2)}) async-start(), calls=%async_computation.4 | async-start | bytes 11796480 | tf_op jit(solution)/shard_map/reduce_scatter | solution.py:282
  13.4 4.5 %collective-permute-start = (bf16[32,4224]{1,0:T(8,128)(2,1)S(1)}, bf16[32,4224]{1,0:T(8,128)(2,1)S(1)}, u32[]{:S(2)}, u32[]{:S(2)}) collective-permute-start(bf16[32,4224]{1,0:T(8,128)(2,1)S(1)} %concatenate.12), channel_id=1, source_target_pairs={{0,1},{1,0},{2,3},{3,2},{4,5},{5,4},{6,7},{7,6},{8,9},{9,8},{10,11... | collective-permute-start | bytes 811016 | tf_op jit(solution)/shard_map/ppermute | solution.py:36
  17.9 10.2 %collective-permute-start.1 = (bf16[64,4224]{1,0:T(8,128)(2,1)S(1)}, bf16[64,4224]{1,0:T(8,128)(2,1)S(1)}, u32[]{:S(2)}, u32[]{:S(2)}) collective-permute-start(bf16[64,4224]{1,0:T(8,128)(2,1)S(1)} %pad_maximum_fusion.1), channel_id=1, source_target_pairs={{0,2},{1,15},{2,4},{3,1},{4,6},{5,3},{6,8},{7,5},{8,10},{9,7},{10,... | collective-permute-start | bytes 1622024 | tf_op jit(solution)/shard_map/ppermute | solution.py:32
  28.1 9.4 %collective-permute-start.2 = (bf16[64,4224]{1,0:T(8,128)(2,1)S(1)}, bf16[64,4224]{1,0:T(8,128)(2,1)S(1)}, u32[]{:S(2)}, u32[]{:S(2)}) collective-permute-start(bf16[64,4224]{1,0:T(8,128)(2,1)S(1)} %collective-permute-done.1), channel_id=1, source_target_pairs={{0,2},{1,15},{2,4},{3,1},{4,6},{5,3},{6,8},{7,5},{8,10},{9,7},{10,... | collective-permute-start | bytes 1622024 | tf_op jit(solution)/shard_map/ppermute | solution.py:32
  37.5 9.8 %collective-permute-start.3 = (bf16[64,4224]{1,0:T(8,128)(2,1)S(1)}, bf16[64,4224]{1,0:T(8,128)(2,1)S(1)}, u32[]{:S(2)}, u32[]{:S(2)}) collective-permute-start(bf16[64,4224]{1,0:T(8,128)(2,1)S(1)} %collective-permute-done.2), channel_id=1, source_target_pairs={{0,2},{1,15},{2,4},{3,1},{4,6},{5,3},{6,8},{7,5},{8,10},{9,7},{10,... | collective-permute-start | bytes 1622024 | tf_op jit(solution)/shard_map/ppermute | solution.py:32
  47.4 11.7 %copy-start.6 = (bf16[64,4224]{1,0:T(8,128)(2,1)}, bf16[64,4224]{1,0:T(8,128)(2,1)S(1)}, u32[]{:S(2)}) copy-start(bf16[64,4224]{1,0:T(8,128)(2,1)S(1)} %collective-permute-done.3) | copy-start | bytes 1622020
  47.4 11.7 %collective-permute-start.4 = (bf16[64,4224]{1,0:T(8,128)(2,1)S(1)}, bf16[64,4224]{1,0:T(8,128)(2,1)S(1)}, u32[]{:S(2)}, u32[]{:S(2)}) collective-permute-start(bf16[64,4224]{1,0:T(8,128)(2,1)S(1)} %collective-permute-done.3), channel_id=1, source_target_pairs={{1,15},{3,1},{5,3},{7,5},{9,7},{11,9},{13,11},{15,13},{17,31},{19,... | collective-permute-start | bytes 1622024 | tf_op jit(solution)/shard_map/ppermute | solution.py:32
  60.4 1.4 copy-start.13
  60.4 1.4 copy-start.14
  60.4 1.4 copy-start.15
  60.4 1.9 copy-start.9
  170.1 5.4 %copy-start.12 = (s32[512]{0:T(512)S(1)}, s32[512]{0:T(512)}, u32[]{:S(2)}) copy-start(s32[512]{0:T(512)} %constant.134.clone) | copy-start | bytes 6148
  170.1 31.8 %all-to-all-start.2 = ((bf16[8,64,2048]{2,1,0:T(8,128)(2,1)}), bf16[8,64,2048]{2,1,0:T(8,128)(2,1)}, u32[]{:S(2)}, u32[]{:S(2)}) async-start(bf16[8,64,2048]{2,1,0:T(8,128)(2,1)} %bitcast.28), calls=%async_computation.2 | async-start | bytes 4194304 | tf_op jit(solution)/shard_map/all_to_all | solution.py:63
  177.9 1.3 copy-start.4
  179.2 29.9 %collective-permute-start.10 = (bf16[64,2048]{1,0:T(8,128)(2,1)S(1)}, bf16[64,2048]{1,0:T(8,128)(2,1)}, u32[]{:S(2)}, u32[]{:S(2)}) collective-permute-start(bf16[64,2048]{1,0:T(8,128)(2,1)S(1)} %slice.241), channel_id=1, source_target_pairs={{1,3},{3,5},{5,7},{7,9},{9,11},{11,13},{13,15},{15,1},{17,19},{19,... | collective-permute-start | bytes 786440 | tf_op jit(solution)/shard_map/ppermute | solution.py:32
  202.0 7.1 %copy-start.5 = (f32[256,2048]{1,0:T(8,128)S(1)}, f32[256,2048]{1,0:T(8,128)}, u32[]{:S(2)}) copy-start(f32[256,2048]{1,0:T(8,128)} %copy-done.4) | copy-start | bytes 6291460
  207.1 9.7 %collective-permute-start.5 = (bf16[64,2176]{1,0:T(8,128)(2,1)S(1)}, bf16[64,2176]{1,0:T(8,128)(2,1)S(1)}, u32[]{:S(2)}, u32[]{:S(2)}) collective-permute-start(bf16[64,2176]{1,0:T(8,128)(2,1)S(1)} %slice.240), channel_id=1, source_target_pairs={{1,3},{3,5},{5,7},{7,9},{9,11},{11,13},{13,15},{15,1},{17,19},{19,... | collective-permute-start | bytes 835592 | tf_op jit(solution)/shard_map/ppermute | solution.py:32
  210.1 9.6 %collective-permute-start.11 = (bf16[64,2048]{1,0:T(8,128)(2,1)S(1)}, bf16[64,2048]{1,0:T(8,128)(2,1)S(1)}, u32[]{:S(2)}, u32[]{:S(2)}) collective-permute-start(bf16[64,2048]{1,0:T(8,128)(2,1)S(1)} %fusion.5), channel_id=1, source_target_pairs={{0,14},{1,3},{2,0},{3,5},{4,2},{5,7},{6,4},{7,9},{8,6},{9,11},{10,... | collective-permute-start | bytes 786440 | tf_op jit(solution)/shard_map/ppermute | solution.py:32
  216.9 7.1 %collective-permute-start.6 = (bf16[64,2176]{1,0:T(8,128)(2,1)S(1)}, bf16[64,2176]{1,0:T(8,128)(2,1)S(1)}, u32[]{:S(2)}, u32[]{:S(2)}) collective-permute-start(bf16[64,2176]{1,0:T(8,128)(2,1)S(1)} %fusion.2), channel_id=1, source_target_pairs={{0,14},{1,3},{2,0},{3,5},{4,2},{5,7},{6,4},{7,9},{8,6},{9,11},{10,... | collective-permute-start | bytes 835592 | tf_op jit(solution)/shard_map/ppermute | solution.py:32
  219.7 7.1 %collective-permute-start.12 = (bf16[64,2048]{1,0:T(8,128)(2,1)S(1)}, bf16[64,2048]{1,0:T(8,128)(2,1)S(1)}, u32[]{:S(2)}, u32[]{:S(2)}) collective-permute-start(bf16[64,2048]{1,0:T(8,128)(2,1)S(1)} %fusion.6), channel_id=1, source_target_pairs={{0,14},{1,3},{2,0},{3,5},{4,2},{5,7},{6,4},{7,9},{8,6},{9,11},{10,... | collective-permute-start | bytes 786440 | tf_op jit(solution)/shard_map/ppermute | solution.py:32
  224.1 6.7 %collective-permute-start.7 = (bf16[64,2176]{1,0:T(8,128)(2,1)S(1)}, bf16[64,2176]{1,0:T(8,128)(2,1)S(1)}, u32[]{:S(2)}, u32[]{:S(2)}) collective-permute-start(bf16[64,2176]{1,0:T(8,128)(2,1)S(1)} %fusion.3), channel_id=1, source_target_pairs={{0,14},{1,3},{2,0},{3,5},{4,2},{5,7},{6,4},{7,9},{8,6},{9,11},{10,... | collective-permute-start | bytes 835592 | tf_op jit(solution)/shard_map/ppermute | solution.py:32
  226.9 6.7 %collective-permute-start.13 = (bf16[64,2048]{1,0:T(8,128)(2,1)S(1)}, bf16[64,2048]{1,0:T(8,128)(2,1)S(1)}, u32[]{:S(2)}, u32[]{:S(2)}) collective-permute-start(bf16[64,2048]{1,0:T(8,128)(2,1)S(1)} %fusion.7), channel_id=1, source_target_pairs={{0,14},{1,3},{2,0},{3,5},{4,2},{5,7},{6,4},{7,9},{8,6},{9,11},{10,... | collective-permute-start | bytes 786440 | tf_op jit(solution)/shard_map/ppermute | solution.py:32
  230.8 6.7 %collective-permute-start.8 = (bf16[64,2176]{1,0:T(8,128)(2,1)S(1)}, bf16[64,2176]{1,0:T(8,128)(2,1)S(1)}, u32[]{:S(2)}, u32[]{:S(2)}) collective-permute-start(bf16[64,2176]{1,0:T(8,128)(2,1)S(1)} %fusion.4), channel_id=1, source_target_pairs={{0,14},{1,3},{2,0},{3,5},{4,2},{5,7},{6,4},{7,9},{8,6},{9,11},{10,... | collective-permute-start | bytes 835592 | tf_op jit(solution)/shard_map/ppermute | solution.py:32
  233.6 4.0 %collective-permute-start.14 = (bf16[32,2048]{1,0:T(8,128)(2,1)S(1)}, bf16[32,2048]{1,0:T(8,128)(2,1)S(1)}, u32[]{:S(2)}, u32[]{:S(2)}) collective-permute-start(bf16[32,2048]{1,0:T(8,128)(2,1)S(1)} %slice.243), channel_id=1, source_target_pairs={{0,1},{1,0},{2,3},{3,2},{4,5},{5,4},{6,7},{7,6},{8,9},{9,8},{10,11... | collective-permute-start | bytes 393224 | tf_op jit(solution)/shard_map/ppermute | solution.py:36
  237.6 1.4 collective-permute-start.9
  240.7 1.7 copy-start
  (2 other events, 1.5 us)
Sparse Core Ops, SparseCore 0:
  12.4 98.3 all-gather.2
  138.4 89.4 reduce-scatter.1

commit v4 on v3

--- a/solution.py
+++ b/solution.py
@@ -86,9 +86,11 @@
     ]
 
 
-def pack_kernel(gate, up, down, packed, sems):
-    for move in copies(pack_moves(gate, up, down, packed), sems):
-        move.wait()
+def pack_kernel(gate, up, down, rest, packed):
+    at = 0
+    for piece in (gate, up, down, rest):
+        packed[:, at : at + piece.shape[1]] = piece[...]
+        at += piece.shape[1]
 
 
 def unpack_kernel(packed, gate, up, down, sems):
@@ -195,9 +197,19 @@
 
 def pack(gate, up, down):
     rows, width = gate.shape
-    return call(pack_kernel, [ANY] * 3, [VMEM], [((rows, 3 * width), BF)], [], 5, 16)(
-        gate, up, down
-    )[0]
+    step, rest = rows // 4, width - rows
+    return pl.pallas_call(
+        pack_kernel,
+        grid=(4,),
+        in_specs=[
+            pl.BlockSpec((step, width), lambda i: (i, 0)),
+            pl.BlockSpec((step, width), lambda i: (i, 0)),
+            pl.BlockSpec((step, rows), lambda i: (i, 0)),
+            pl.BlockSpec((step, rest), lambda i: (4 + i % 2, i // 2)),
+        ],
+        out_specs=pl.BlockSpec((step, 3 * width), lambda i: (i, 0)),
+        out_shape=jax.ShapeDtypeStruct((rows, 3 * width), BF),
+    )(gate, up, down, down)
 
 
 def unpack(packed):

time: 251 us -> 250 us (level)
  local copies, waits for them, and re-layouts: 9.98 us -> 6.61 us
    unnamed x34 -> x28, local copies, waits for them, and re-layouts: 7.73 us -> 4.36 us
where the time goes in v4:
time: 250 us; the launch traced here: 249 us
  blocking collectives  85.4 us (34%)
  waiting for transfers between devices  73.7 us (29%)
  Pallas kernels  30.3 us (12%)
  starting transfers between devices  29.6 us (12%)
  between operations  14.5 us (6%)
  local copies, waits for them, and re-layouts  6.61 us (3%)
  matrix products  5.24 us (2%)
  other arithmetic  4.12 us (2%)
    all_to_all x2, blocking collectives, swap_rows(): lax.all_to_all(value, 'expert', 0, 0, axis_index_groups=XC_PLANES, tiled=...  85.4 us
    ppermute x12, waiting for transfers between devices, along_z(): return lax.ppermute(value, 'expert', pairs)  51.2 us
    all_to_all x1, waiting for transfers between devices, swap_rows(): lax.all_to_all(value, 'expert', 0, 0, axis_index_groups=XC_PLANES, tiled=...  20.6 us
    ppermute x12, starting transfers between devices, along_z(): return lax.ppermute(value, 'expert', pairs)  20.6 us
    pallas_call x1, Pallas kernels, body(): call(expert_kernel, [ANY] * 2, [ANY, ANY, ANY], [((slots, width), BF), ((...  19.9 us
    all_to_all x1, starting transfers between devices, swap_rows(): lax.all_to_all(value, 'expert', 0, 0, axis_index_groups=XC_PLANES, tiled=...  5.38 us
    dot_general x5, matrix products, dot(): lax.dot_general(left_side, right_side, (((left_dim,), (right_dim,)), ((),...  5.24 us
    pallas_call x1, Pallas kernels, body(): call(combine_kernel, [ANY, ANY, VMEM, VMEM, VMEM], [VMEM], [((held, width...  5.11 us
  transfers between devices with their start and end apart: 18, of which 14 were waited for; matrix products, arithmetic and copies ran while one was open for 5% of the time, Pallas kernels for 2%

profile of v4, /device:TPU:1, one launch (start us, length us, event | category | flops | bytes accessed | tf_op | source)
XLA Modules:
  0.0 249.5 jit_solution(7186375571981245772)
XLA Ops:
  7.2 3.9 %shard_map.154 = bf16[512,2304]{1,0:T(8,128)(2,1)} custom-call(bf16[512,768]{1,0:T(8,128)(2,1)} %bitcast.29, bf16[512,768]{1,0:T(8,128)(2,1)} %bitcast.30, bf16[768,512]{1,0:T(8,128)(2,1)} %bitcast.25, bf16[768,512]{1,0:T(8,128)(2,1)} %bitcast.26), custom_call_target="tpu_custom_call" | custom-call | tf_op jit(solution)/shard_map/pallas_call | solution.py:201
  12.2 3.3 %collective-permute-start = (bf16[32,4224]{1,0:T(8,128)(2,1)S(1)}, bf16[32,4224]{1,0:T(8,128)(2,1)S(1)}, u32[]{:S(2)}, u32[]{:S(2)}) collective-permute-start(bf16[32,4224]{1,0:T(8,128)(2,1)S(1)} %concatenate.12), channel_id=1, source_target_pairs={{0,1},{1,0},{2,3},{3,2},{4,5},{5,4},{6,7},{7,6},{8,9},{9,8},{10,11... | collective-permute-start | bytes 811016 | tf_op jit(solution)/shard_map/ppermute | solution.py:36
  15.5 1.2 collective-permute-done
  16.8 3.9 %collective-permute-start.1 = (bf16[64,4224]{1,0:T(8,128)(2,1)S(1)}, bf16[64,4224]{1,0:T(8,128)(2,1)S(1)}, u32[]{:S(2)}, u32[]{:S(2)}) collective-permute-start(bf16[64,4224]{1,0:T(8,128)(2,1)S(1)} %pad_maximum_fusion.1), channel_id=1, source_target_pairs={{0,2},{1,15},{2,4},{3,1},{4,6},{5,3},{6,8},{7,5},{8,10},{9,7},{10,... | collective-permute-start | bytes 1622024 | tf_op jit(solution)/shard_map/ppermute | solution.py:32
  20.7 6.3 %collective-permute-done.1 = bf16[64,4224]{1,0:T(8,128)(2,1)S(1)} collective-permute-done((bf16[64,4224]{1,0:T(8,128)(2,1)S(1)}, bf16[64,4224]{1,0:T(8,128)(2,1)S(1)}, u32[]{:S(2)}, u32[]{:S(2)}) %collective-permute-start.1) | collective-permute-done | bytes 540704 | tf_op jit(solution)/shard_map/ppermute | solution.py:32
  27.0 3.1 %collective-permute-start.2 = (bf16[64,4224]{1,0:T(8,128)(2,1)S(1)}, bf16[64,4224]{1,0:T(8,128)(2,1)S(1)}, u32[]{:S(2)}, u32[]{:S(2)}) collective-permute-start(bf16[64,4224]{1,0:T(8,128)(2,1)S(1)} %collective-permute-done.1), channel_id=1, source_target_pairs={{0,2},{1,15},{2,4},{3,1},{4,6},{5,3},{6,8},{7,5},{8,10},{9,7},{10,... | collective-permute-start | bytes 1622024 | tf_op jit(solution)/shard_map/ppermute | solution.py:32
  30.1 6.3 %collective-permute-done.2 = bf16[64,4224]{1,0:T(8,128)(2,1)S(1)} collective-permute-done((bf16[64,4224]{1,0:T(8,128)(2,1)S(1)}, bf16[64,4224]{1,0:T(8,128)(2,1)S(1)}, u32[]{:S(2)}, u32[]{:S(2)}) %collective-permute-start.2) | collective-permute-done | bytes 540704 | tf_op jit(solution)/shard_map/ppermute | solution.py:32
  36.4 3.5 %collective-permute-start.3 = (bf16[64,4224]{1,0:T(8,128)(2,1)S(1)}, bf16[64,4224]{1,0:T(8,128)(2,1)S(1)}, u32[]{:S(2)}, u32[]{:S(2)}) collective-permute-start(bf16[64,4224]{1,0:T(8,128)(2,1)S(1)} %collective-permute-done.2), channel_id=1, source_target_pairs={{0,2},{1,15},{2,4},{3,1},{4,6},{5,3},{6,8},{7,5},{8,10},{9,7},{10,... | collective-permute-start | bytes 1622024 | tf_op jit(solution)/shard_map/ppermute | solution.py:32
  39.9 6.3 %collective-permute-done.3 = bf16[64,4224]{1,0:T(8,128)(2,1)S(1)} collective-permute-done((bf16[64,4224]{1,0:T(8,128)(2,1)S(1)}, bf16[64,4224]{1,0:T(8,128)(2,1)S(1)}, u32[]{:S(2)}, u32[]{:S(2)}) %collective-permute-start.3) | collective-permute-done | bytes 540704 | tf_op jit(solution)/shard_map/ppermute | solution.py:32
  46.2 5.4 %collective-permute-start.4 = (bf16[64,4224]{1,0:T(8,128)(2,1)S(1)}, bf16[64,4224]{1,0:T(8,128)(2,1)S(1)}, u32[]{:S(2)}, u32[]{:S(2)}) collective-permute-start(bf16[64,4224]{1,0:T(8,128)(2,1)S(1)} %collective-permute-done.3), channel_id=1, source_target_pairs={{1,15},{3,1},{5,3},{7,5},{9,7},{11,9},{13,11},{15,13},{17,31},{19,... | collective-permute-start | bytes 1622024 | tf_op jit(solution)/shard_map/ppermute | solution.py:32
  51.7 6.2 %collective-permute-done.4 = bf16[64,4224]{1,0:T(8,128)(2,1)S(1)} collective-permute-done((bf16[64,4224]{1,0:T(8,128)(2,1)S(1)}, bf16[64,4224]{1,0:T(8,128)(2,1)S(1)}, u32[]{:S(2)}, u32[]{:S(2)}) %collective-permute-start.4) | collective-permute-done | bytes 540704 | tf_op jit(solution)/shard_map/ppermute | solution.py:32
  58.1 1.2 pad_maximum_fusion.sources
  62.3 1.3 multiply_convert_fusion
  63.6 53.6 %all_to_all.34 = bf16[8,64,4096]{2,1,0:T(8,128)(2,1)} all-to-all(bf16[8,64,4096]{2,1,0:T(8,128)(2,1)S(1)} %bitcast.24), channel_id=1, replica_groups={{0,1,16,17,32,33,48,49},{2,3,18,19,34,35,50,51},{4,5,20,21,36,37,52,53}..., dimensions={0} | all-to-all | bytes 8388608 | tf_op jit(solution)/shard_map/all_to_all | solution.py:63
  117.2 19.9 %shard_map.155 = (bf16[512,2048]{1,0:T(8,128)(2,1)}, bf16[512,2048]{1,0:T(8,128)(2,1)}, bf16[2048,2304]{1,0:T(8,128)(2,1)}) custom-call(bf16[512,4096]{1,0:T(8,128)(2,1)} %bitcast.21, bf16[4,512,2304]{2,1,0:T(8,128)(2,1)} %bitcast.22), custom_call_target="tpu_custom_call" | custom-call | flops 1 | bytes 1 | tf_op jit(solution)/shard_map/pallas_call | solution.py:274
  137.2 31.8 %all_to_all.35 = bf16[8,64,2048]{2,1,0:T(8,128)(2,1)} all-to-all(bf16[8,64,2048]{2,1,0:T(8,128)(2,1)} %bitcast.28), channel_id=1, replica_groups={{0,1,16,17,32,33,48,49},{2,3,18,19,34,35,50,51},{4,5,20,21,36,37,52,53}..., dimensions={0} | all-to-all | bytes 4194304 | tf_op jit(solution)/shard_map/all_to_all | solution.py:63
  169.0 5.4 %all-to-all-start.2 = ((bf16[8,64,2048]{2,1,0:T(8,128)(2,1)}), bf16[8,64,2048]{2,1,0:T(8,128)(2,1)}, u32[]{:S(2)}, u32[]{:S(2)}) async-start(bf16[8,64,2048]{2,1,0:T(8,128)(2,1)} %bitcast.27), calls=%async_computation.2 | async-start | bytes 4194304 | tf_op jit(solution)/shard_map/all_to_all | solution.py:63
  174.4 2.3 fusion.90
  176.7 1.3 copy-done.1
  178.0 1.9 collective-permute-start.10
  180.2 20.6 %all-to-all-done.2 = bf16[8,64,2048]{2,1,0:T(8,128)(2,1)} async-done(((bf16[8,64,2048]{2,1,0:T(8,128)(2,1)}), bf16[8,64,2048]{2,1,0:T(8,128)(2,1)}, u32[]{:S(2)}, u32[]{:S(2)}) %all-to-all-start.2) | async-done | bytes 2097184 | tf_op jit(solution)/shard_map/all_to_all | solution.py:63
  200.8 5.1 %shard_map.156 = f32[256,2176]{1,0:T(8,128)S(1)} custom-call(bf16[512,2048]{1,0:T(8,128)(2,1)} %bitcast.10.back, bf16[256,4224]{1,0:T(8,128)(2,1)S(1)} %pad_maximum_fusion.sources, f32[256,512]{1,0:T(8,128)S(1)} %convolution_select_fusion.weights, bf16[256,512]{1,0:T(8,128)(2,1)S(1)} %get-tuple-element.55.select, f32[512,128]{1,0:T(8,128)S(1)} %compare_convert_fusion.place), custom_call_target="tpu_custom_call" | custom-call | flops 1 | bytes 1 | tf_op jit(solution)/shard_map/pallas_call | solution.py:301
  206.0 1.9 collective-permute-start.5
  209.3 6.4 %collective-permute-done.5 = bf16[64,2176]{1,0:T(8,128)(2,1)S(1)} collective-permute-done((bf16[64,2176]{1,0:T(8,128)(2,1)S(1)}, bf16[64,2176]{1,0:T(8,128)(2,1)S(1)}, u32[]{:S(2)}, u32[]{:S(2)}) %collective-permute-start.5) | collective-permute-done | bytes 278560 | tf_op jit(solution)/shard_map/ppermute | solution.py:32
  215.9 2.7 %collective-permute-done.11 = bf16[64,2048]{1,0:T(8,128)(2,1)S(1)} collective-permute-done((bf16[64,2048]{1,0:T(8,128)(2,1)S(1)}, bf16[64,2048]{1,0:T(8,128)(2,1)S(1)}, u32[]{:S(2)}, u32[]{:S(2)}) %collective-permute-start.11) | collective-permute-done | bytes 262176 | tf_op jit(solution)/shard_map/ppermute | solution.py:32
  218.7 4.2 %collective-permute-done.6 = bf16[64,2176]{1,0:T(8,128)(2,1)S(1)} collective-permute-done((bf16[64,2176]{1,0:T(8,128)(2,1)S(1)}, bf16[64,2176]{1,0:T(8,128)(2,1)S(1)}, u32[]{:S(2)}, u32[]{:S(2)}) %collective-permute-start.6) | collective-permute-done | bytes 278560 | tf_op jit(solution)/shard_map/ppermute | solution.py:32
  223.0 2.7 %collective-permute-done.12 = bf16[64,2048]{1,0:T(8,128)(2,1)S(1)} collective-permute-done((bf16[64,2048]{1,0:T(8,128)(2,1)S(1)}, bf16[64,2048]{1,0:T(8,128)(2,1)S(1)}, u32[]{:S(2)}, u32[]{:S(2)}) %collective-permute-start.12) | collective-permute-done | bytes 262176 | tf_op jit(solution)/shard_map/ppermute | solution.py:32
  225.8 3.8 %collective-permute-done.7 = bf16[64,2176]{1,0:T(8,128)(2,1)S(1)} collective-permute-done((bf16[64,2176]{1,0:T(8,128)(2,1)S(1)}, bf16[64,2176]{1,0:T(8,128)(2,1)S(1)}, u32[]{:S(2)}, u32[]{:S(2)}) %collective-permute-start.7) | collective-permute-done | bytes 278560 | tf_op jit(solution)/shard_map/ppermute | solution.py:32
  229.8 2.7 %collective-permute-done.13 = bf16[64,2048]{1,0:T(8,128)(2,1)S(1)} collective-permute-done((bf16[64,2048]{1,0:T(8,128)(2,1)S(1)}, bf16[64,2048]{1,0:T(8,128)(2,1)S(1)}, u32[]{:S(2)}, u32[]{:S(2)}) %collective-permute-start.13) | collective-permute-done | bytes 262176 | tf_op jit(solution)/shard_map/ppermute | solution.py:32
  232.6 3.7 %collective-permute-done.8 = bf16[64,2176]{1,0:T(8,128)(2,1)S(1)} collective-permute-done((bf16[64,2176]{1,0:T(8,128)(2,1)S(1)}, bf16[64,2176]{1,0:T(8,128)(2,1)S(1)}, u32[]{:S(2)}, u32[]{:S(2)}) %collective-permute-start.8) | collective-permute-done | bytes 278560 | tf_op jit(solution)/shard_map/ppermute | solution.py:32
  239.5 1.7 copy-done
  241.2 1.4 shard_map.157
  (81 shorter events, 10.0 us)
Async XLA Ops:
  7.2 110.1 %all-gather.3.cloned.1.call-start = ((), (), s32[]{:S(2)}) async-start(), calls=%async_computation.5 | async-start | bytes 11796480 | tf_op jit(solution)/shard_map/all_gather | solution.py:237
  11.1 0.7 copy-start.7
  11.1 0.8 copy-start.8
  11.1 1.0 copy-start.4
  11.1 1.0 copy-start.5
  11.2 228.4 %reduce-scatter.2.cloned.1.call-start = ((), (), s32[]{:S(2)}) async-start(), calls=%async_computation.4 | async-start | bytes 11796480 | tf_op jit(solution)/shard_map/reduce_scatter | solution.py:294
  12.2 4.5 %collective-permute-start = (bf16[32,4224]{1,0:T(8,128)(2,1)S(1)}, bf16[32,4224]{1,0:T(8,128)(2,1)S(1)}, u32[]{:S(2)}, u32[]{:S(2)}) collective-permute-start(bf16[32,4224]{1,0:T(8,128)(2,1)S(1)} %concatenate.12), channel_id=1, source_target_pairs={{0,1},{1,0},{2,3},{3,2},{4,5},{5,4},{6,7},{7,6},{8,9},{9,8},{10,11... | collective-permute-start | bytes 811016 | tf_op jit(solution)/shard_map/ppermute | solution.py:36
  16.8 10.2 %collective-permute-start.1 = (bf16[64,4224]{1,0:T(8,128)(2,1)S(1)}, bf16[64,4224]{1,0:T(8,128)(2,1)S(1)}, u32[]{:S(2)}, u32[]{:S(2)}) collective-permute-start(bf16[64,4224]{1,0:T(8,128)(2,1)S(1)} %pad_maximum_fusion.1), channel_id=1, source_target_pairs={{0,2},{1,15},{2,4},{3,1},{4,6},{5,3},{6,8},{7,5},{8,10},{9,7},{10,... | collective-permute-start | bytes 1622024 | tf_op jit(solution)/shard_map/ppermute | solution.py:32
  27.0 9.4 %collective-permute-start.2 = (bf16[64,4224]{1,0:T(8,128)(2,1)S(1)}, bf16[64,4224]{1,0:T(8,128)(2,1)S(1)}, u32[]{:S(2)}, u32[]{:S(2)}) collective-permute-start(bf16[64,4224]{1,0:T(8,128)(2,1)S(1)} %collective-permute-done.1), channel_id=1, source_target_pairs={{0,2},{1,15},{2,4},{3,1},{4,6},{5,3},{6,8},{7,5},{8,10},{9,7},{10,... | collective-permute-start | bytes 1622024 | tf_op jit(solution)/shard_map/ppermute | solution.py:32
  36.4 9.8 %collective-permute-start.3 = (bf16[64,4224]{1,0:T(8,128)(2,1)S(1)}, bf16[64,4224]{1,0:T(8,128)(2,1)S(1)}, u32[]{:S(2)}, u32[]{:S(2)}) collective-permute-start(bf16[64,4224]{1,0:T(8,128)(2,1)S(1)} %collective-permute-done.2), channel_id=1, source_target_pairs={{0,2},{1,15},{2,4},{3,1},{4,6},{5,3},{6,8},{7,5},{8,10},{9,7},{10,... | collective-permute-start | bytes 1622024 | tf_op jit(solution)/shard_map/ppermute | solution.py:32
  46.2 11.7 %copy-start.3 = (bf16[64,4224]{1,0:T(8,128)(2,1)}, bf16[64,4224]{1,0:T(8,128)(2,1)S(1)}, u32[]{:S(2)}) copy-start(bf16[64,4224]{1,0:T(8,128)(2,1)S(1)} %collective-permute-done.3) | copy-start | bytes 1622020
  46.2 11.7 %collective-permute-start.4 = (bf16[64,4224]{1,0:T(8,128)(2,1)S(1)}, bf16[64,4224]{1,0:T(8,128)(2,1)S(1)}, u32[]{:S(2)}, u32[]{:S(2)}) collective-permute-start(bf16[64,4224]{1,0:T(8,128)(2,1)S(1)} %collective-permute-done.3), channel_id=1, source_target_pairs={{1,15},{3,1},{5,3},{7,5},{9,7},{11,9},{13,11},{15,13},{17,31},{19,... | collective-permute-start | bytes 1622024 | tf_op jit(solution)/shard_map/ppermute | solution.py:32
  59.3 1.4 copy-start.10
  59.3 1.4 copy-start.11
  59.3 1.4 copy-start.12
  59.3 1.9 copy-start.6
  169.0 5.4 %copy-start.9 = (s32[512]{0:T(512)S(1)}, s32[512]{0:T(512)}, u32[]{:S(2)}) copy-start(s32[512]{0:T(512)} %constant.134.clone) | copy-start | bytes 6148
  169.0 31.8 %all-to-all-start.2 = ((bf16[8,64,2048]{2,1,0:T(8,128)(2,1)}), bf16[8,64,2048]{2,1,0:T(8,128)(2,1)}, u32[]{:S(2)}, u32[]{:S(2)}) async-start(bf16[8,64,2048]{2,1,0:T(8,128)(2,1)} %bitcast.27), calls=%async_computation.2 | async-start | bytes 4194304 | tf_op jit(solution)/shard_map/all_to_all | solution.py:63
  176.7 1.3 copy-start.1
  178.0 29.9 %collective-permute-start.10 = (bf16[64,2048]{1,0:T(8,128)(2,1)S(1)}, bf16[64,2048]{1,0:T(8,128)(2,1)}, u32[]{:S(2)}, u32[]{:S(2)}) collective-permute-start(bf16[64,2048]{1,0:T(8,128)(2,1)S(1)} %slice.241), channel_id=1, source_target_pairs={{1,3},{3,5},{5,7},{7,9},{9,11},{11,13},{13,15},{15,1},{17,19},{19,... | collective-permute-start | bytes 786440 | tf_op jit(solution)/shard_map/ppermute | solution.py:32
  200.8 7.1 %copy-start.2 = (f32[256,2048]{1,0:T(8,128)S(1)}, f32[256,2048]{1,0:T(8,128)}, u32[]{:S(2)}) copy-start(f32[256,2048]{1,0:T(8,128)} %copy-done.1) | copy-start | bytes 6291460
  206.0 9.7 %collective-permute-start.5 = (bf16[64,2176]{1,0:T(8,128)(2,1)S(1)}, bf16[64,2176]{1,0:T(8,128)(2,1)S(1)}, u32[]{:S(2)}, u32[]{:S(2)}) collective-permute-start(bf16[64,2176]{1,0:T(8,128)(2,1)S(1)} %slice.240), channel_id=1, source_target_pairs={{1,3},{3,5},{5,7},{7,9},{9,11},{11,13},{13,15},{15,1},{17,19},{19,... | collective-permute-start | bytes 835592 | tf_op jit(solution)/shard_map/ppermute | solution.py:32
  209.0 9.6 %collective-permute-start.11 = (bf16[64,2048]{1,0:T(8,128)(2,1)S(1)}, bf16[64,2048]{1,0:T(8,128)(2,1)S(1)}, u32[]{:S(2)}, u32[]{:S(2)}) collective-permute-start(bf16[64,2048]{1,0:T(8,128)(2,1)S(1)} %fusion.5), channel_id=1, source_target_pairs={{0,14},{1,3},{2,0},{3,5},{4,2},{5,7},{6,4},{7,9},{8,6},{9,11},{10,... | collective-permute-start | bytes 786440 | tf_op jit(solution)/shard_map/ppermute | solution.py:32
  215.8 7.1 %collective-permute-start.6 = (bf16[64,2176]{1,0:T(8,128)(2,1)S(1)}, bf16[64,2176]{1,0:T(8,128)(2,1)S(1)}, u32[]{:S(2)}, u32[]{:S(2)}) collective-permute-start(bf16[64,2176]{1,0:T(8,128)(2,1)S(1)} %fusion.2), channel_id=1, source_target_pairs={{0,14},{1,3},{2,0},{3,5},{4,2},{5,7},{6,4},{7,9},{8,6},{9,11},{10,... | collective-permute-start | bytes 835592 | tf_op jit(solution)/shard_map/ppermute | solution.py:32
  218.6 7.1 %collective-permute-start.12 = (bf16[64,2048]{1,0:T(8,128)(2,1)S(1)}, bf16[64,2048]{1,0:T(8,128)(2,1)S(1)}, u32[]{:S(2)}, u32[]{:S(2)}) collective-permute-start(bf16[64,2048]{1,0:T(8,128)(2,1)S(1)} %fusion.6), channel_id=1, source_target_pairs={{0,14},{1,3},{2,0},{3,5},{4,2},{5,7},{6,4},{7,9},{8,6},{9,11},{10,... | collective-permute-start | bytes 786440 | tf_op jit(solution)/shard_map/ppermute | solution.py:32
  222.9 6.7 %collective-permute-start.7 = (bf16[64,2176]{1,0:T(8,128)(2,1)S(1)}, bf16[64,2176]{1,0:T(8,128)(2,1)S(1)}, u32[]{:S(2)}, u32[]{:S(2)}) collective-permute-start(bf16[64,2176]{1,0:T(8,128)(2,1)S(1)} %fusion.3), channel_id=1, source_target_pairs={{0,14},{1,3},{2,0},{3,5},{4,2},{5,7},{6,4},{7,9},{8,6},{9,11},{10,... | collective-permute-start | bytes 835592 | tf_op jit(solution)/shard_map/ppermute | solution.py:32
  225.7 6.7 %collective-permute-start.13 = (bf16[64,2048]{1,0:T(8,128)(2,1)S(1)}, bf16[64,2048]{1,0:T(8,128)(2,1)S(1)}, u32[]{:S(2)}, u32[]{:S(2)}) collective-permute-start(bf16[64,2048]{1,0:T(8,128)(2,1)S(1)} %fusion.7), channel_id=1, source_target_pairs={{0,14},{1,3},{2,0},{3,5},{4,2},{5,7},{6,4},{7,9},{8,6},{9,11},{10,... | collective-permute-start | bytes 786440 | tf_op jit(solution)/shard_map/ppermute | solution.py:32
  229.7 6.7 %collective-permute-start.8 = (bf16[64,2176]{1,0:T(8,128)(2,1)S(1)}, bf16[64,2176]{1,0:T(8,128)(2,1)S(1)}, u32[]{:S(2)}, u32[]{:S(2)}) collective-permute-start(bf16[64,2176]{1,0:T(8,128)(2,1)S(1)} %fusion.4), channel_id=1, source_target_pairs={{0,14},{1,3},{2,0},{3,5},{4,2},{5,7},{6,4},{7,9},{8,6},{9,11},{10,... | collective-permute-start | bytes 835592 | tf_op jit(solution)/shard_map/ppermute | solution.py:32
  232.5 4.0 %collective-permute-start.14 = (bf16[32,2048]{1,0:T(8,128)(2,1)S(1)}, bf16[32,2048]{1,0:T(8,128)(2,1)S(1)}, u32[]{:S(2)}, u32[]{:S(2)}) collective-permute-start(bf16[32,2048]{1,0:T(8,128)(2,1)S(1)} %slice.243), channel_id=1, source_target_pairs={{0,1},{1,0},{2,3},{3,2},{4,5},{5,4},{6,7},{7,6},{8,9},{9,8},{10,11... | collective-permute-start | bytes 393224 | tf_op jit(solution)/shard_map/ppermute | solution.py:36
  236.4 1.4 collective-permute-start.9
  239.5 1.7 copy-start
Sparse Core Ops, SparseCore 0:
  11.3 98.3 all-gather.2
  137.3 89.5 reduce-scatter.1
